TPU v7x, 512 devices: a whole 4x8x8 slice. The times are simulated.
512 devices in a mesh: row: 128 (over y, z_lo, x, core), col: 4 (over z_hi).
Axes of the slice: x: 4, y: 8, z: 8 (z_hi: 4, z_lo: 2; z = z_hi * 2 + z_lo), core: 2. Of those that a mesh axis runs over, the one named last changes fastest.
Arguments:
- tokens: bfloat16 [512, 128, 256], P('row', 'col'), may hold values from -6 to 6
- gain: float32 [256], replicated, may hold values from 0.25 to 1.75
- w_qkv: bfloat16 [256, 768], replicated, may hold values from -0.375 to 0.375
- head_scale: float32 [4], replicated, may hold values from 3 to 12
- w_out: bfloat16 [256, 256], replicated, may hold values from -0.375 to 0.375
- w_merge: bfloat16 [1024, 512], replicated, may hold values from -0.1875 to 0.1875
- d_merged: bfloat16 [256, 64, 512], P('row', 'col'), may hold values from -0.25 to 0.25
- d_skip: bfloat16 [512, 128, 256], P('row', 'col'), may hold values from -0.25 to 0.25
Outputs:
- skip_out: bfloat16 [512, 128, 256], P('row', 'col')
- merged: bfloat16 [256, 64, 512], P('row', 'col')
- grad_tokens: bfloat16 [512, 128, 256], P('row', 'col')
- grad_qkv: float32 [256, 768], P('row', 'col')
- grad_out: float32 [256, 256], P('row', 'col')
- grad_merge: float32 [1024, 512], P('row', 'col')
- grad_gain: float32 [256], replicated
- grad_scale: float32 [4], replicated
All inputs are finite; a program needn't handle non-finite values.
Results may differ from a plain program's by a relative error of at most 0.012.
The roundings to bfloat16 on the way count: a program that leaves them out, or rounds other values in their place, can miss the bound.
Values may be sent and summed in bfloat16 or wider, within the bound.
A program may use at most 64 MiB of HBM per device.

v0:
```python
import jax
import jax.numpy as jnp
import numpy as np
from jax import lax
from jax.sharding import PartitionSpec as P

RADIUS = 3
TILE_R = 4
TILE_C = 16
IMG_MAX = 512


EPS = 1e-06


def extended(value, sides, width):
    for axis, dim in sides:
        count, length = (lax.axis_size(axis), value.shape[dim])
        up = [(i, (i + 1) % count) for i in range(count - 1)]
        down = [(j, i) for i, j in up]
        last = lax.slice_in_dim(value, length - width, length, axis=dim)
        initial = lax.slice_in_dim(value, 0, width, axis=dim)
        before = lax.ppermute(last, axis, up)
        after = lax.ppermute(initial, axis, down)
        value = jnp.concatenate([before, value, after], axis=dim)
    return value


def passed_along(value, axis, steps):
    count = lax.axis_size(axis)
    initial, last = (max(0, -steps), min(count, count - steps))
    return lax.ppermute(value, axis, [(source, source + steps) for source in range(initial, last)])


def split_queries(block):
    rows, cols, feats = block.shape
    part = block.reshape(rows // TILE_R, TILE_R, cols // TILE_C, TILE_C, feats).transpose(
        0, 2, 1, 3, 4
    )
    return part.reshape(rows // TILE_R, cols // TILE_C, TILE_R * TILE_C, feats)


def join_queries(tiles, rows, cols):
    feats = tiles.shape[-1]
    part = tiles.reshape(rows // TILE_R, cols // TILE_C, TILE_R, TILE_C, feats).transpose(
        0, 2, 1, 3, 4
    )
    return part.reshape(rows, cols, feats)


def cut_block(padded, cols):
    span_r = TILE_R + 2 * RADIUS
    span_c = TILE_C + 2 * RADIUS
    feats = padded.shape[-1]
    count = cols // TILE_C
    parts = [padded[:, j * TILE_C : j * TILE_C + span_c] for j in range(count)]
    return jnp.stack(parts, axis=0).reshape(1, count, span_r * span_c, feats)


def add_block(tiles, cols):
    span_r = TILE_R + 2 * RADIUS
    span_c = TILE_C + 2 * RADIUS
    feats = tiles.shape[-1]
    count = cols // TILE_C
    pieces = tiles.reshape(count, span_r, span_c, feats)
    total = jnp.zeros((span_r, cols + 2 * RADIUS, feats), tiles.dtype)
    for j in range(count):
        total = total.at[:, j * TILE_C : j * TILE_C + span_c].add(pieces[j])
    return total


def window_mask():
    span_c = TILE_C + 2 * RADIUS
    count = (TILE_R + 2 * RADIUS) * span_c
    query_r = np.arange(TILE_R * TILE_C) // TILE_C
    query_c = np.arange(TILE_R * TILE_C) % TILE_C
    key_r = np.arange(count) // span_c
    key_c = np.arange(count) % span_c
    diff_r = key_r[None, :] - query_r[:, None]
    diff_c = key_c[None, :] - query_c[:, None]
    return jnp.asarray(
        (diff_r >= 0) & (diff_r <= 2 * RADIUS) & (diff_c >= 0) & (diff_c <= 2 * RADIUS)
    )


def attend(q_tiles, kv_tiles, valid_tiles, heads):
    nrow, ncol, nq, width = q_tiles.shape
    nk = kv_tiles.shape[2]
    dim = width // heads
    query = q_tiles.reshape(nrow, ncol, nq, heads, dim)
    keys = kv_tiles[..., :width].reshape(nrow, ncol, nk, heads, dim)
    values = kv_tiles[..., width:].reshape(nrow, ncol, nk, heads, dim)
    scores = jnp.einsum("abqhe,abkhe->abhqk", query, keys, preferred_element_type=jnp.float32)
    allowed = window_mask()[None, None, None] & valid_tiles[:, :, None, None, :]
    expo = jnp.where(allowed, jnp.exp(scores), 0.0)
    prob = expo / jnp.sum(expo, axis=-1, keepdims=True)
    weights = prob.astype(jnp.bfloat16)
    out = jnp.einsum("abhqk,abkhe->abqhe", weights, values, preferred_element_type=jnp.float32)
    return (out.reshape(nrow, ncol, nq, width).astype(jnp.bfloat16), prob)


def attend_back(q_tiles, kv_tiles, prob, grad_tiles, heads):
    nrow, ncol, nq, width = q_tiles.shape
    nk = kv_tiles.shape[2]
    dim = width // heads
    query = q_tiles.reshape(nrow, ncol, nq, heads, dim)
    keys = kv_tiles[..., :width].reshape(nrow, ncol, nk, heads, dim)
    values = kv_tiles[..., width:].reshape(nrow, ncol, nk, heads, dim)
    grads = grad_tiles.reshape(nrow, ncol, nq, heads, dim)
    d_weights = jnp.einsum("abqhe,abkhe->abhqk", grads, values, preferred_element_type=jnp.float32)
    d_scores = prob * (d_weights - jnp.sum(d_weights * prob, axis=-1, keepdims=True))
    score_grad = d_scores.astype(jnp.bfloat16)
    weights = prob.astype(jnp.bfloat16)
    d_query = jnp.einsum("abhqk,abkhe->abqhe", score_grad, keys, preferred_element_type=jnp.float32)
    d_keys = jnp.einsum("abhqk,abqhe->abkhe", score_grad, query, preferred_element_type=jnp.float32)
    d_values = jnp.einsum("abhqk,abqhe->abkhe", weights, grads, preferred_element_type=jnp.float32)
    kv_grad = jnp.concatenate(
        [d_keys.reshape(nrow, ncol, nk, width), d_values.reshape(nrow, ncol, nk, width)], axis=-1
    )
    return (d_query.reshape(nrow, ncol, nq, width), kv_grad)


def on_device(tokens, gain, w_qkv, head_scale, w_out, w_merge, d_merged, d_skip):
    rows, cols, width = tokens.shape
    heads = head_scale.shape[0]
    head_dim = width // heads
    x = tokens.astype(jnp.float32)
    inverse = lax.rsqrt(jnp.mean(x * x, axis=-1, keepdims=True) + EPS)
    normed = (x * inverse * gain).astype(jnp.bfloat16)
    flat_normed = normed.reshape(rows * cols, width)
    qkv = jnp.dot(flat_normed, w_qkv, preferred_element_type=jnp.float32).reshape(
        rows, cols, 3, heads, head_dim
    )
    query, key_raw, value = (qkv[:, :, 0], qkv[:, :, 1], qkv[:, :, 2])
    q_norm = lax.rsqrt(jnp.sum(query * query, axis=-1, keepdims=True) + EPS)
    k_norm = lax.rsqrt(jnp.sum(key_raw * key_raw, axis=-1, keepdims=True) + EPS)
    q_unit = query * q_norm
    k_unit = key_raw * k_norm
    q_hat = (q_unit * head_scale[:, None]).reshape(rows, cols, width).astype(jnp.bfloat16)
    kv = jnp.concatenate(
        [k_unit.reshape(rows, cols, width), value.reshape(rows, cols, width)], axis=-1
    ).astype(jnp.bfloat16)
    kv_pad = extended(kv, (("row", 0), ("col", 1)), RADIUS)
    image_rows = min(IMG_MAX, rows * lax.axis_size("row"))
    row_start = lax.axis_index("row") * rows
    col_start = lax.axis_index("col") * cols
    first = row_start // image_rows * image_rows
    grid_r = jnp.arange(rows + 2 * RADIUS, dtype=jnp.int32) + row_start - RADIUS
    grid_c = jnp.arange(cols + 2 * RADIUS, dtype=jnp.int32) + col_start - RADIUS
    inside_r = (grid_r >= first) & (grid_r < first + image_rows)
    inside_c = (grid_c >= 0) & (grid_c < cols * lax.axis_size("col"))
    inside = inside_r[:, None] & inside_c[None, :]
    starts = jnp.arange(rows // TILE_R, dtype=jnp.int32) * TILE_R

    def pieces(start):
        q_tiles = split_queries(q_hat)
        kv_tiles = cut_block(kv_pad, cols)
        valid_tiles = cut_block(inside[:, :, None], cols)[..., 0]
        return (q_tiles, kv_tiles, valid_tiles)

    def forward_rows(start):
        q_tiles, kv_tiles, valid_tiles = pieces(start)
        out, prob = attend(q_tiles, kv_tiles, valid_tiles, heads)
        return join_queries(out, TILE_R, cols)

    attn = lax.map(forward_rows, starts).reshape(rows, cols, width)
    flat_attn = attn.reshape(rows * cols, width)
    proj = jnp.dot(flat_attn, w_out, preferred_element_type=jnp.float32).reshape(rows, cols, width)
    skip_out = (x + proj).astype(jnp.bfloat16)
    merge_in = skip_out.reshape(rows // 2, 2, cols // 2, 2, width).transpose(0, 2, 1, 3, 4)
    merge_in = merge_in.reshape(rows // 2 * (cols // 2), 4 * width)
    merged = jnp.dot(merge_in, w_merge, preferred_element_type=jnp.float32).astype(jnp.bfloat16)
    merged = merged.reshape(rows // 2, cols // 2, w_merge.shape[1])
    flat_dm = d_merged.reshape(rows // 2 * (cols // 2), d_merged.shape[-1])
    grad_merge = jnp.dot(merge_in.T, flat_dm, preferred_element_type=jnp.float32)
    d_in = jnp.dot(flat_dm, w_merge.T, preferred_element_type=jnp.float32)
    d_in = (
        d_in.reshape(rows // 2, cols // 2, 2, 2, width)
        .transpose(0, 2, 1, 3, 4)
        .reshape(rows, cols, width)
    )
    d_y = d_skip.astype(jnp.float32) + d_in
    dy_b = d_y.astype(jnp.bfloat16).reshape(rows * cols, width)
    grad_out = jnp.dot(flat_attn.T, dy_b, preferred_element_type=jnp.float32)
    d_attn = (
        jnp.dot(dy_b, w_out.T, preferred_element_type=jnp.float32)
        .astype(jnp.bfloat16)
        .reshape(rows, cols, width)
    )

    def backward_rows(start):
        q_tiles, kv_tiles, valid_tiles = pieces(start)
        out, prob = attend(q_tiles, kv_tiles, valid_tiles, heads)
        d_q_tiles, d_kv_tiles = attend_back(q_tiles, kv_tiles, prob, split_queries(d_attn), heads)
        d_kv_block = add_block(d_kv_tiles, cols)
        top = d_kv_block[:RADIUS]
        middle = d_kv_block[RADIUS : RADIUS + TILE_R]
        bottom = d_kv_block[RADIUS + TILE_R :]
        return (join_queries(d_q_tiles, TILE_R, cols), top, middle, bottom)

    d_qrows, top, middle, bottom = lax.map(backward_rows, starts)
    d_qhat = d_qrows.reshape(rows, cols, width)
    top_next = jnp.concatenate([top[1:], jnp.zeros_like(top)], axis=0)
    bottom_prev = jnp.concatenate([jnp.zeros_like(bottom), bottom[:-1]], axis=0)
    full = middle + jnp.pad(top_next, ((0, 0), (TILE_R - RADIUS, 0), (0, 0), (0, 0)))
    full = full + jnp.pad(bottom_prev, ((0, 0), (0, TILE_R - RADIUS), (0, 0), (0, 0)))
    full = full.reshape(rows, cols + 2 * RADIUS, 2 * width)
    d_kv_pad = jnp.concatenate([top[0], full, bottom[-1]], axis=0)
    left_rim = d_kv_pad[:, :RADIUS]
    right_rim = d_kv_pad[:, RADIUS + cols :]
    inner = d_kv_pad[:, RADIUS : RADIUS + cols]
    from_right = passed_along(left_rim.astype(jnp.bfloat16), "col", -1).astype(left_rim.dtype)
    from_left = passed_along(right_rim.astype(jnp.bfloat16), "col", 1).astype(right_rim.dtype)
    inner = inner.at[:, cols - RADIUS :].add(from_right)
    inner = inner.at[:, :RADIUS].add(from_left)
    top_rim = inner[:RADIUS]
    bottom_rim = inner[RADIUS + rows :]
    d_kv = inner[RADIUS : RADIUS + rows]
    from_below = passed_along(top_rim.astype(jnp.bfloat16), "row", -1).astype(top_rim.dtype)
    from_above = passed_along(bottom_rim.astype(jnp.bfloat16), "row", 1).astype(bottom_rim.dtype)
    d_kv = d_kv.at[rows - RADIUS :].add(from_below)
    d_kv = d_kv.at[:RADIUS].add(from_above)
    g_qhat = d_qhat.reshape(rows, cols, heads, head_dim)
    local_scale = jnp.sum(q_unit * g_qhat, axis=(0, 1, 3))
    g_unit = g_qhat * head_scale[:, None]
    d_query = q_norm * (g_unit - q_unit * jnp.sum(q_unit * g_unit, axis=-1, keepdims=True))
    g_key = d_kv[:, :, :width].reshape(rows, cols, heads, head_dim)
    d_key = k_norm * (g_key - k_unit * jnp.sum(k_unit * g_key, axis=-1, keepdims=True))
    d_value = d_kv[:, :, width:].reshape(rows, cols, heads, head_dim)
    d_qkv = (
        jnp.stack([d_query, d_key, d_value], axis=2)
        .reshape(rows * cols, 3 * width)
        .astype(jnp.bfloat16)
    )
    grad_qkv = jnp.dot(flat_normed.T, d_qkv, preferred_element_type=jnp.float32)
    d_normed = jnp.dot(d_qkv, w_qkv.T, preferred_element_type=jnp.float32).reshape(
        rows, cols, width
    )
    local_gain = jnp.sum(x * inverse * d_normed, axis=(0, 1))
    scaled = gain * d_normed
    g_x = inverse * scaled - x * inverse**3 * jnp.mean(x * scaled, axis=-1, keepdims=True)
    grad_tokens = (d_y + g_x).astype(jnp.bfloat16)
    partial_sums = (
        lax.psum_scatter(grad_qkv, "row", scatter_dimension=0, tiled=True),
        lax.psum_scatter(grad_out, "row", scatter_dimension=0, tiled=True),
        lax.psum_scatter(grad_merge, "row", scatter_dimension=0, tiled=True),
    )
    summed = (
        lax.psum_scatter(partial_sums[0], "col", scatter_dimension=1, tiled=True),
        lax.psum_scatter(partial_sums[1], "col", scatter_dimension=1, tiled=True),
        lax.psum_scatter(partial_sums[2], "col", scatter_dimension=1, tiled=True),
    )
    grad_gain, grad_scale = lax.psum((local_gain, local_scale), ("row", "col"))
    return (skip_out, merged, grad_tokens, summed[0], summed[1], summed[2], grad_gain, grad_scale)


def solution(mesh):
    return jax.shard_map(
        on_device,
        mesh=mesh,
        in_specs=(
            P("row", "col", None),
            P(),
            P(),
            P(),
            P(),
            P(),
            P("row", "col", None),
            P("row", "col", None),
        ),
        out_specs=(
            P("row", "col", None),
            P("row", "col", None),
            P("row", "col", None),
            P("row", "col"),
            P("row", "col"),
            P("row", "col"),
            P(),
            P(),
        ),
        check_vma=False,
    )
```

profile of v0, /device:TPU:6, one launch (start us, length us, event | category | flops | bytes accessed | tf_op | source)
XLA Modules:
  0.0 1852.3 jit_solution(2060805952163278679)
XLA Ops:
  7.2 1.0 fusion.26
  8.8 1.2 copy.113
  10.0 0.9 fusion.24
  12.9 2.1 collective-permute-start
  14.9 3.6 collective-permute-start.1
  20.9 0.7 fusion.38
  21.7 1.3 collective-permute-start.3
  23.0 6.7 collective-permute-start.2
  30.2 0.8 copy.133
  32.1 1.3 fusion.19
  33.4 0.9 fusion.1
  34.2 1.0 multiply_reduce_fusion
  35.2 1.1 fusion.33
  36.3 1.7 copy.123
  38.0 1.7 convert_element_type.115
  39.7 0.8 copy.124
  41.1 1.7 fusion.53
  42.9 1.0 copy.136
  43.8 0.8 multiply_convert_fusion
  44.7 1.2 fusion.51
  45.8 1.0 copy.135
  46.8 2.1 pad_maximum_fusion.1
  48.9 1.1 reshape.587
  50.0 1.1 add.162
  51.6 1.3 collective-permute-start.4
  52.9 8.1 collective-permute-start.5
  61.4 1.2 collective-permute-done.5
  63.1 0.6 fusion.49
  63.7 1.9 collective-permute-start.6
  66.3 0.8 reshape_reshape.14
  67.3 3.2 collective-permute-start.7
  70.5 0.9 fusion.21
  71.4 1.8 collective-permute-done.7
  74.3 1.0 fusion.17
  75.9 1.2 fusion.52
  77.5 1.8 fusion.54
  79.4 1.3 dynamic-slice.51
  81.6 0.9 convolution_convert_fusion.2
  83.2 1081.3 %all-reduce.9.cloned.1.call-done = (f32[256,768]{1,0:T(8,128)}, f32[256,256]{1,0:T(8,128)}) async-done(((f32[256,768]{1,0:T(8,128)}, f32[256,256]{1,0:T(8,128)}), (f32[256,768]{1,0:T(8,128)}, f32[256,256]{1,0:T(8,128)})) %all-reduce.9.cloned.1.call-update) | async-done | bytes 1048592
  1164.5 0.7 constant_dynamic-slice_fusion
  1165.2 0.8 copy.147
  1166.1 0.8 constant_dynamic-slice_fusion.1
  1166.8 0.9 copy.145
  1167.8 562.0 %reduce-scatter.9.cloned.1.call-done = f32[8,512]{1,0:T(8,128)} async-done(((f32[1024,512]{1,0:T(8,128)}), f32[8,512]{1,0:T(8,128)}) %reduce-scatter.9.cloned.1.call-update) | async-done | bytes 16400 | tf_op jit(solution)/shard_map/reduce_scatter | solution.py:246
  1729.9 0.8 fusion.30
  1730.7 112.1 %all-reduce.5 = (f32[256]{0:T(256)}, f32[4]{0:T(128)}) all-reduce(f32[256]{0:T(256)S(1)} %get-tuple-element.142, f32[4]{0:T(128)S(1)} %reduce_sum.121), channel_id=1, replica_groups=mesh['row'=128,'col'=4] {'row','col'}, use_global_device_ids=true, to_apply=%region_16.17 | all-reduce | flops 260 | bytes 2080 | tf_op jit(solution)/shard_map/psum | solution.py:253
  1842.8 1.4 copy.148
  1844.2 1.5 copy.146
  (166 shorter events, 11.9 us)
Async XLA Ops:
  7.2 12.0 copy-start
  7.2 1157.3 %all-reduce.9.cloned.1.call-start = ((), (), s32[]{:S(2)}) async-start(), calls=%async_computation.8 | async-start | bytes 2097152
  8.8 2.1 copy-start.21
  11.0 0.6 copy-start.8
  11.6 7.0 copy-start.26
  11.6 7.5 copy-start.23
  11.6 7.6 copy-start.19
  12.8 7.9 copy-start.17
  12.8 7.9 copy-start.14
  12.9 8.8 collective-permute-start
  14.9 6.7 collective-permute-start.1
  20.7 10.2 copy-start.12
  21.7 9.2 collective-permute-start.3
  23.0 8.4 collective-permute-start.2
  30.0 4.2 copy-start.4
  31.9 1.4 copy-start.5
  40.5 0.6 copy-start.10
  44.7 2.1 copy-start.1
  51.6 9.5 collective-permute-start.4
  52.9 12.7 copy-start.6
  52.9 9.7 collective-permute-start.5
  63.7 6.8 collective-permute-start.6
  66.2 7.6 copy-start.27
  67.3 5.9 collective-permute-start.7
  71.4 2.4 copy-start.7
  73.8 2.1 copy-start.9
  75.3 1.9 copy-start.2
  75.3 1.9 copy-start.11
  75.3 1.9 copy-start.15
  75.4 2.1 copy-start.20
  77.1 1652.8 %reduce-scatter.9.cloned.1.call-start = ((), (), s32[]{:S(2)}) async-start(), calls=%async_computation.4 | async-start | bytes 2113536 | tf_op jit(solution)/shard_map/reduce_scatter | solution.py:246
  77.3 2.0 copy-start.16
  77.5 3.9 copy-start.13
  79.3 3.5 copy-start.3
  79.3 3.5 copy-start.22
  79.3 3.5 copy-start.24
  79.3 1650.6 %copy-start.18 = (bf16[4,32,256]{2,1,0:T(8,128)(2,1)S(1)}, bf16[4,32,256]{2,1,0:T(8,128)(2,1)}, u32[]{:S(2)}) copy-start(bf16[4,32,256]{2,1,0:T(8,128)(2,1)} %param.29) | copy-start | bytes 196612
  79.3 1650.6 %copy-start.25 = (f32[4,32]{1,0:T(4,128)S(1)}, f32[4,32]{1,0:T(4,128)}, u32[]{:S(2)}) copy-start(f32[4,32]{1,0:T(4,128)} %get-tuple-element.170) | copy-start | bytes 1540
  79.3 1763.5 %reduce-scatter.15.cloned.1.call-start = ((), (), s32[]{:S(2)}) async-start(), calls=%async_computation.7 | async-start | bytes 163840
  1166.0 678.2 %reduce-scatter.13.cloned.1.call-start = ((), (), s32[]{:S(2)}) async-start(), calls=%async_computation.6 | async-start | bytes 491520
  1167.8 678.0 %reduce-scatter.11.cloned.1.call-start = ((), (), s32[]{:S(2)}) async-start(), calls=%async_computation.5 | async-start | bytes 20480 | tf_op jit(solution)/shard_map/reduce_scatter | solution.py:251
Sparse Core Ops, SparseCore 0:
  77.2 1087.2 all-reduce.8
  1167.5 562.3 reduce-scatter.8
  1732.7 41.7 reduce-scatter.14
  1777.4 27.6 reduce-scatter.12
  1808.3 26.5 reduce-scatter.10
where the time goes:
time: 1860 us; the launch traced here: 1850 us
  waiting for transfers between devices  1650 us (89%)
  blocking collectives  112 us (6%)
  starting transfers between devices  28.3 us (2%)
  local copies, waits for them, and re-layouts  26.3 us (1%)
    unnamed x8, waiting for transfers between devices  1080 us
    reduce_scatter x1, waiting for transfers between devices, on_device(): lax.psum_scatter(grad_merge, 'row', scatter_dimension=0, tiled=True)  562 us
    psum x1, blocking collectives, on_device(): grad_gain, grad_scale = lax.psum((local_gain, local_scale), ('row', 'col'))  112 us
  transfers between devices with their start and end apart: 13, of which 5 were waited for; matrix products, arithmetic and copies ran while one was open for 1% of the time, Pallas kernels for 0%

commit v1 on v0

--- a/solution.py
+++ b/solution.py
@@ -2,6 +2,8 @@
 import jax.numpy as jnp
 import numpy as np
 from jax import lax
+from jax.experimental import pallas as pl
+from jax.experimental.pallas import tpu as pltpu
 from jax.sharding import PartitionSpec as P
 
 RADIUS = 3
@@ -11,6 +13,210 @@
 
 
 EPS = 1e-06
+
+
+MESH = pl.DeviceIdType.MESH
+NX, NY, NZ = 4, 8, 8
+F32, BF16 = jnp.float32, jnp.bfloat16
+
+
+def place():
+    row, col = lax.axis_index("row"), lax.axis_index("col")
+    return row // 16, (row // 8) % 2, (row // 2) % 4, row % 2, col
+
+
+def device(y, zl, x, core, col):
+    return (((y * 2 + zl) * 4 + x) * 2 + core, col)
+
+
+def peers():
+    y, zl, x, core, col = place()
+    z = col * 2 + zl
+    out = {"core": (core, [(1 - core, device(y, zl, x, 1 - core, col))])}
+    out["x"] = (x, [])
+    for p in range(1, NX):
+        t = (x + p) % NX
+        out["x"][1].append((t, device(y, zl, t, core, col)))
+    out["y"] = (y, [])
+    for p in range(1, NY):
+        t = (y + p) % NY
+        out["y"][1].append((t, device(t, zl, x, core, col)))
+    out["z"] = (z, [])
+    for p in range(1, NZ):
+        t = (z + p) % NZ
+        out["z"][1].append((t, device(y, t % 2, x, core, t // 2)))
+    return out
+
+
+def start_copies(copies):
+    for c in copies:
+        c.start()
+    return copies
+
+
+def wait_copies(copies):
+    for c in copies:
+        c.wait()
+
+
+def exchange(peer_list, source, slots, send, recv):
+    return start_copies(
+        [
+            pltpu.make_async_remote_copy(
+                src_ref=source(t),
+                dst_ref=slots.at[p],
+                send_sem=send.at[p],
+                recv_sem=recv.at[p],
+                device_id=dev,
+                device_id_type=MESH,
+            )
+            for p, (t, dev) in enumerate(peer_list)
+        ]
+    )
+
+
+def spread(mine, peer_list, slots, send, recv):
+    return start_copies(
+        [
+            pltpu.make_async_remote_copy(
+                src_ref=slots.at[mine],
+                dst_ref=slots.at[mine],
+                send_sem=send.at[p],
+                recv_sem=recv.at[p],
+                device_id=dev,
+                device_id_type=MESH,
+            )
+            for p, (t, dev) in enumerate(peer_list)
+        ]
+    )
+
+
+def rows_at(ref, index, size):
+    return ref.at[:, pl.ds(pl.multiple_of(index * size, size), size), :]
+
+def reduce_kernel(ga, gb, gs, perm, o_qkv, o_out, o_merge, o_gs,
+                  sa1, ra1, sa2, ra2, sa3, ra3, sa4, ra4,
+                  sb1, rb1, sb2, rb2, sb3, rb3, sb4, rb4,
+                  g1, g2, g3, g4, tsem_a, tsem_b, tsem_g):
+    near = peers()
+    bar = pltpu.get_barrier_semaphore()
+    for axis in ("core", "x", "y", "z"):
+        for _, dev in near[axis][1]:
+            pl.semaphore_signal(bar, inc=1, device_id=dev, device_id_type=MESH)
+    core, x, y, z = (near[a][0] for a in ("core", "x", "y", "z"))
+    sa1[...] = ga[:, pl.ds(pl.multiple_of((1 - core) * 128, 128), 128), :].astype(BF16)
+    sb1[...] = gb[:, pl.ds(pl.multiple_of((1 - core) * 512, 512), 512), :].astype(BF16)
+    g1[core] = gs[...]
+    pl.semaphore_wait(bar, 1 + 3 + 7 + 7)
+
+    def sems(table, stage):
+        return table.at[0, pl.ds(7 * stage, 7)], table.at[1, pl.ds(7 * stage, 7)]
+
+    ca = exchange(near["core"][1], lambda t: sa1, ra1, *sems(tsem_a, 0))
+    cg = spread(core, near["core"][1], g1, *sems(tsem_g, 0))
+    cb = exchange(near["core"][1], lambda t: sb1, rb1, *sems(tsem_b, 0))
+
+    wait_copies(ca)
+    sa2[...] = (ga[:, pl.ds(pl.multiple_of(core * 128, 128), 128), :] + ra1[0].astype(F32)).astype(BF16)
+    ca = exchange(near["x"][1], lambda t: rows_at(sa2, t, 32), ra2, *sems(tsem_a, 1))
+    wait_copies(cg)
+    g2[x] = g1[0] + g1[1]
+    cg = spread(x, near["x"][1], g2, *sems(tsem_g, 1))
+    wait_copies(cb)
+    sb2[...] = (gb[:, pl.ds(pl.multiple_of(core * 512, 512), 512), :] + rb1[0].astype(F32)).astype(BF16)
+    cb = exchange(near["x"][1], lambda t: rows_at(sb2, t, 128), rb2, *sems(tsem_b, 1))
+
+    wait_copies(ca)
+    total = sa2[:, pl.ds(pl.multiple_of(x * 32, 32), 32), :].astype(F32)
+    for p in range(3):
+        total = total + ra2[p].astype(F32)
+    sa3[...] = jnp.dot(perm[...], total.astype(BF16).reshape(128, 256), preferred_element_type=F32).astype(BF16).reshape(8, 16, 256)
+    ca = exchange(near["y"][1], lambda t: sa3.at[t], ra3, *sems(tsem_a, 2))
+    wait_copies(cg)
+    g3[y] = (g2[0] + g2[1]) + (g2[2] + g2[3])
+    cg = spread(y, near["y"][1], g3, *sems(tsem_g, 2))
+    wait_copies(cb)
+    total = sb2[:, pl.ds(pl.multiple_of(x * 128, 128), 128), :].astype(F32)
+    for p in range(3):
+        total = total + rb2[p].astype(F32)
+    sb3[...] = total.astype(BF16)
+    cb = exchange(near["y"][1], lambda t: rows_at(sb3, t, 16), rb3, *sems(tsem_b, 2))
+
+    wait_copies(ca)
+    total = sa3[y].astype(F32)
+    for p in range(7):
+        total = total + ra3[p].astype(F32)
+    sa4[...] = total.reshape(2, 8, 256)
+    ca = exchange(near["z"][1], lambda t: sa4.at[t // 4], ra4, *sems(tsem_a, 3))
+    wait_copies(cg)
+    g4[z] = ((g3[0] + g3[1]) + (g3[2] + g3[3])) + ((g3[4] + g3[5]) + (g3[6] + g3[7]))
+    cg = spread(z, near["z"][1], g4, *sems(tsem_g, 3))
+    wait_copies(cb)
+    total = sb3[:, pl.ds(pl.multiple_of(y * 16, 16), 16), :].astype(F32)
+    for p in range(7):
+        total = total + rb3[p].astype(F32)
+    sb4[...] = total
+    cb = exchange(near["z"][1], lambda t: sb4.at[t // 2, pl.ds(pl.multiple_of(t % 2 * 8, 8), 8), :], rb4, *sems(tsem_b, 3))
+
+    wait_copies(ca)
+    total = sa4[z // 4]
+    for p in range(7):
+        total = total + ra4[p]
+    part = z % 4
+    piece = jnp.zeros((2, 256), F32)
+    for k in range(4):
+        piece = piece + jnp.where(part == k, total[2 * k : 2 * k + 2], 0.0)
+    o_qkv[...] = piece[:, :192]
+    o_out[...] = piece[:, 192:]
+    wait_copies(cg)
+    o_gs[...] = ((g4[0] + g4[1]) + (g4[2] + g4[3])) + ((g4[4] + g4[5]) + (g4[6] + g4[7]))
+    wait_copies(cb)
+    total = sb4[z // 2, pl.ds(pl.multiple_of(z % 2 * 8, 8), 8), :]
+    for p in range(7):
+        total = total + rb4[p]
+    o_merge[...] = total
+
+
+def slab_order():
+    perm = np.zeros((128, 128), np.float32)
+    for c in range(4):
+        for yy in range(8):
+            for k in range(4):
+                perm[yy * 16 + c * 4 + k, c * 32 + yy * 4 + k] = 1
+    return jnp.asarray(perm, BF16)
+
+
+def reduce_all(grad_qkv, grad_out, grad_merge, gain, scale):
+    a = jnp.concatenate([grad_qkv.reshape(256, 4, 192), grad_out.reshape(256, 4, 64)], axis=-1)
+    a = a.reshape(8, 2, 4, 2, 2, 4, 256).transpose(5, 3, 2, 0, 1, 4, 6).reshape(4, 256, 256)
+    b = grad_merge.reshape(8, 2, 4, 2, 8, 4, 128).transpose(5, 3, 2, 0, 1, 4, 6).reshape(4, 1024, 128)
+    gs = jnp.concatenate([gain, scale, jnp.zeros(764, F32)]).reshape(8, 128)
+    vmem = pl.BlockSpec(memory_space=pltpu.VMEM)
+    V = pltpu.VMEM
+    return pl.pallas_call(
+        reduce_kernel,
+        out_shape=(
+            jax.ShapeDtypeStruct((2, 192), F32),
+            jax.ShapeDtypeStruct((2, 64), F32),
+            jax.ShapeDtypeStruct((8, 128), F32),
+            jax.ShapeDtypeStruct((8, 128), F32),
+        ),
+        in_specs=[vmem] * 4,
+        out_specs=(vmem,) * 4,
+        scratch_shapes=[
+            V((4, 128, 256), BF16), V((1, 4, 128, 256), BF16),
+            V((4, 128, 256), BF16), V((3, 4, 32, 256), BF16),
+            V((8, 16, 256), BF16), V((7, 16, 256), BF16),
+            V((2, 8, 256), F32), V((7, 8, 256), F32),
+            V((4, 512, 128), BF16), V((1, 4, 512, 128), BF16),
+            V((4, 512, 128), BF16), V((3, 4, 128, 128), BF16),
+            V((4, 128, 128), BF16), V((7, 4, 16, 128), BF16),
+            V((4, 16, 128), F32), V((7, 8, 128), F32),
+            V((2, 8, 128), F32), V((4, 8, 128), F32), V((8, 8, 128), F32), V((8, 8, 128), F32),
+            pltpu.SemaphoreType.DMA((2, 28)), pltpu.SemaphoreType.DMA((2, 28)), pltpu.SemaphoreType.DMA((2, 28)),
+        ],
+        compiler_params=pltpu.CompilerParams(collective_id=0, has_side_effects=True, vmem_limit_bytes=48 * 2**20),
+    )(a, b, gs, slab_order())
 
 
 def extended(value, sides, width):
@@ -240,18 +446,9 @@
     scaled = gain * d_normed
     g_x = inverse * scaled - x * inverse**3 * jnp.mean(x * scaled, axis=-1, keepdims=True)
     grad_tokens = (d_y + g_x).astype(jnp.bfloat16)
-    partial_sums = (
-        lax.psum_scatter(grad_qkv, "row", scatter_dimension=0, tiled=True),
-        lax.psum_scatter(grad_out, "row", scatter_dimension=0, tiled=True),
-        lax.psum_scatter(grad_merge, "row", scatter_dimension=0, tiled=True),
-    )
-    summed = (
-        lax.psum_scatter(partial_sums[0], "col", scatter_dimension=1, tiled=True),
-        lax.psum_scatter(partial_sums[1], "col", scatter_dimension=1, tiled=True),
-        lax.psum_scatter(partial_sums[2], "col", scatter_dimension=1, tiled=True),
-    )
-    grad_gain, grad_scale = lax.psum((local_gain, local_scale), ("row", "col"))
-    return (skip_out, merged, grad_tokens, summed[0], summed[1], summed[2], grad_gain, grad_scale)
+    o_qkv, o_out, o_merge, o_gs = reduce_all(grad_qkv, grad_out, grad_merge, local_gain, local_scale)
+    flat = o_gs.reshape(-1)
+    return (skip_out, merged, grad_tokens, o_qkv, o_out, o_merge, flat[:256], flat[256:260])
 
 
 def solution(mesh):

time: 1860 us -> 135 us (0.07)
  waiting for transfers between devices: 1650 us -> 2.49 us
  blocking collectives: 112 us -> 0 us
  Pallas kernels: 0 us -> 45.4 us
    unnamed x8 -> x0, waiting for transfers between devices: 1080 us -> none
    reduce_scatter x2 -> x0, waiting for transfers between devices: 562 us -> none  [the longest x1 562 us: on_device(): lax.psum_scatter(grad_merge, 'row', scatter_dimension=0, tiled=True)]
    psum x1 -> x0, blocking collectives: 112 us -> none  [on_device(): grad_gain, grad_scale = lax.psum((local_gain, local_scale), ('row', 'col'))]
    pallas_call x0 -> x1, Pallas kernels: none -> 45.4 us  [reduce_all(): pl.pallas_call(reduce_kernel, out_shape=(jax.ShapeDtypeStruct((2, 192), F...]
  transfers between devices with their start and end apart: 13 -> 8, of which waited for: 5 -> 2; matrix products, arithmetic and copies ran while one was open for 1% -> 10% of each run, Pallas kernels for 0% -> 0%
where the time goes in v1:
time: 135 us; the launch traced here: 132 us
  Pallas kernels  45.4 us (34%)
  local copies, waits for them, and re-layouts  33 us (24%)
  starting transfers between devices  28.6 us (21%)
  other arithmetic  11.1 us (8%)
  matrix products  9.61 us (7%)
  waiting for transfers between devices  2.49 us (2%)
  between operations  1.63 us (1%)
    pallas_call x1, Pallas kernels, reduce_all(): pl.pallas_call(reduce_kernel, out_shape=(jax.ShapeDtypeStruct((2, 192), F...  45.4 us
    ppermute x4, starting transfers between devices, passed_along(): lax.ppermute(value, axis, [(source, source + steps) for source in range(i...  14.9 us
    ppermute x2, starting transfers between devices, extended(): before = lax.ppermute(last, axis, up)  8.77 us
    unnamed x66, local copies, waits for them, and re-layouts  5.08 us
    ppermute x2, starting transfers between devices, extended(): after = lax.ppermute(initial, axis, down)  4.93 us
    reshape x1, local copies, waits for them, and re-layouts, reduce_all(): a.reshape(8, 2, 4, 2, 2, 4, 256).transpose(5, 3, 2, 0, 1, 4, 6)  2.98 us
    transpose x1, local copies, waits for them, and re-layouts, reduce_all(): a.reshape(8, 2, 4, 2, 2, 4, 256).transpose(5, 3, 2, 0, 1, 4, 6)  2.75 us
  transfers between devices with their start and end apart: 8, of which 2 were waited for; matrix products, arithmetic and copies ran while one was open for 10% of the time, Pallas kernels for 0%

profile of v1, /device:TPU:6, one launch (start us, length us, event | category | flops | bytes accessed | tf_op | source)
XLA Modules:
  0.0 131.9 jit_solution(3928518370778544863)
XLA Ops:
  0.6 1.0 fusion.26
  1.7 0.6 multiply_multiply_fusion
  2.3 1.2 copy.101
  3.4 0.9 fusion.24
  5.0 0.6 copy-done.3
  6.9 2.1 %collective-permute-start = (bf16[3,32,512]{2,1,0:T(8,128)(2,1)S(1)}, bf16[3,32,512]{2,1,0:T(8,128)(2,1)S(1)}, u32[]{:S(2)}, u32[]{:S(2)}) collective-permute-start(bf16[3,32,512]{2,1,0:T(8,128)(2,1)S(1)} %get-tuple-element.172), channel_id=1, source_target_pairs={{0,4},{4,8},{8,12},{12,16},{16,20},{20,24},{24,28},{28,32},{32,36}... | collective-permute-start | bytes 294920 | tf_op jit(solution)/shard_map/ppermute | solution.py:229
  8.9 3.6 %collective-permute-start.1 = (bf16[3,32,512]{2,1,0:T(8,128)(2,1)S(1)}, bf16[3,32,512]{2,1,0:T(8,128)(2,1)S(1)}, u32[]{:S(2)}, u32[]{:S(2)}) collective-permute-start(bf16[3,32,512]{2,1,0:T(8,128)(2,1)S(1)} %get-tuple-element.173), channel_id=1, source_target_pairs={{4,0},{8,4},{12,8},{16,12},{20,16},{24,20},{28,24},{32,28},{36,32}... | collective-permute-start | bytes 294920 | tf_op jit(solution)/shard_map/ppermute | solution.py:230
  15.0 0.7 fusion.38
  15.7 1.3 collective-permute-start.3
  17.0 6.7 %collective-permute-start.2 = (bf16[10,3,512]{2,1,0:T(4,128)(2,1)S(1)}, bf16[10,3,512]{2,1,0:T(4,128)(2,1)S(1)}, u32[]{:S(2)}, u32[]{:S(2)}) collective-permute-start(bf16[10,3,512]{2,1,0:T(4,128)(2,1)S(1)} %get-tuple-element.171), channel_id=1, source_target_pairs={{0,1},{1,2},{2,3},{4,5},{5,6},{6,7},{8,9},{9,10},{10,11},{12,13},{... | collective-permute-start | bytes 92168 | tf_op jit(solution)/shard_map/ppermute | solution.py:229
  23.8 0.6 dot_general.111
  24.7 0.7 copy.132
  27.7 0.9 convolution_bitcast_fusion.1
  29.5 0.9 convolution_convert_fusion.2
  30.4 0.8 copy.135
  32.4 1.3 collective-permute-start.4
  33.7 0.9 fusion.54
  34.6 1.7 %convolution_bitcast_fusion = f32[4,2,4,8,2,8,128]{6,5,0,1,2,4,3:T(8,128)} fusion(bf16[8,2,4,2,8,32,1]{5,4,6,3,2,1,0:T(8,128)(2,1)S(1)} %bitcast.182, bf16[4,128,32,1,1,1,1]{1,0,2,6,5,4,3:T(4,128)(2,1)S(1)} %bitcast.198), kind=kOutput, calls=%fused_computation | convolution fusion | flops 33554432 | bytes 2195456 | tf_op jit(solution)/shard_map/dot_general | solution.py:381
  36.8 0.8 reshape_reshape.14
  37.8 7.9 %collective-permute-start.5 = (bf16[10,3,512]{2,1,0:T(4,128)(2,1)S(1)}, bf16[10,3,512]{2,1,0:T(4,128)(2,1)S(1)}, u32[]{:S(2)}, u32[]{:S(2)}) collective-permute-start(bf16[10,3,512]{2,1,0:T(4,128)(2,1)S(1)} %get-tuple-element.164), channel_id=1, source_target_pairs={{0,1},{1,2},{2,3},{4,5},{5,6},{6,7},{8,9},{9,10},{10,11},{12,13},{... | collective-permute-start | bytes 92168 | tf_op jit(solution)/shard_map/ppermute | solution.py:238
  46.1 1.2 collective-permute-done.5
  47.8 0.8 fusion.50
  48.5 1.9 %collective-permute-start.6 = (bf16[3,32,512]{2,1,0:T(8,128)(2,1)}, bf16[3,32,512]{2,1,0:T(8,128)(2,1)}, u32[]{:S(2)}, u32[]{:S(2)}) collective-permute-start(bf16[3,32,512]{2,1,0:T(8,128)(2,1)} %get-tuple-element.167), channel_id=1, source_target_pairs={{4,0},{8,4},{12,8},{16,12},{20,16},{24,20},{28,24},{32,28},{36,32}... | collective-permute-start | bytes 294920 | tf_op jit(solution)/shard_map/ppermute | solution.py:238
  50.6 0.6 reduce_sum.121
  51.2 1.9 %copy.137 = f32[4,2,4,8,2,8,128]{6,5,4,3,2,1,0:T(8,128)S(1)} copy(f32[4,2,4,8,2,8,128]{6,5,0,1,2,4,3:T(8,128)} %convolution_bitcast_fusion) | data formatting | bytes 4194304 | tf_op jit(solution)/shard_map/transpose | solution.py:192
  53.2 3.8 %collective-permute-start.7 = (bf16[3,32,512]{2,1,0:T(8,128)(2,1)S(1)}, bf16[3,32,512]{2,1,0:T(8,128)(2,1)S(1)}, u32[]{:S(2)}, u32[]{:S(2)}) collective-permute-start(bf16[3,32,512]{2,1,0:T(8,128)(2,1)S(1)} %get-tuple-element.166), channel_id=1, source_target_pairs={{0,4},{4,8},{8,12},{12,16},{16,20},{20,24},{24,28},{28,32},{32,36}... | collective-permute-start | bytes 294920 | tf_op jit(solution)/shard_map/ppermute | solution.py:238
  57.0 0.9 fusion.21
  57.9 1.2 collective-permute-done.7
  59.2 0.6 slice.340
  59.8 0.8 reshape.607
  60.7 0.9 reshape.606
  61.5 1.0 stack_reshape.3
  62.5 1.6 %fusion.11 = (f32[4,32,4]{1,2,0:T(4,128)S(1)}, f32[4,32,4]{1,2,0:T(4,128)S(1)}) fusion(f32[4,32,4,64]{3,2,1,0:T(4,128)} %reshape_reshape.14, f32[4]{0:T(128)} %param.26, f32[4,32,4]{1,2,0:T(4,128)S(1)} %get-tuple-element.181, f32[4,32,3,4,64]{4,1,3,2,0:T(8,128)} %copy-done.3, f32[4,32,4,64]{3,2,1,0:T(4,128)} %reshape.607, f32[4,32,4]{1,2,0:T(4,128)S(1)} %get-tuple-element.182), kind=kLoop, calls=%fused_computation.32 | loop fusion | flops 228352 | bytes 532496 | tf_op jit(solution)/shard_map/reduce_sum | solution.py:432
  64.1 1.5 %fusion.17 = (bf16[4,32,1,4,64]{4,1,3,2,0:T(8,128)(2,1)S(1)}, bf16[4,32,1,4,64]{4,1,3,2,0:T(8,128)(2,1)S(1)}) fusion(f32[4,32,1,4,64]{4,3,1,0,2:T(4,128)S(1)} %reshape_reshape.13, f32[4,32,4]{1,2,0:T(4,128)S(1)} %get-tuple-element.146, f32[4]{0:T(128)} %param.26, f32[4,32,4]{1,2,0:T(4,128)S(1)} %get-tuple-element.181, f32[4,32,3,4,64]{4,1,3,2,0:T(8,128)} %copy-done.3, ...), kind=kLoop, calls=%fused_computation.43 | loop fusion | flops 360448 | bytes 663568 | tf_op jit(solution)/shard_map/mul | solution.py:432
  65.9 0.9 convert_element_type.124
  66.8 0.9 convert_element_type.122
  67.8 1.5 %fusion.25 = (f32[256]{0:T(256)S(1)}, f32[4,32]{1,0:T(4,128)S(1)}, f32[4,32,256]{2,1,0:T(8,128)S(1)}) fusion(bf16[4,32,256]{2,1,0:T(8,128)(2,1)} %param.23, f32[4,32]{1,0:T(4,128)} %copy-done.22, f32[256]{0:T(256)} %param.24, bf16[4,32,768]{2,1,0:T(8,128)(2,1)} %convert_element_type.122, bf16[256,768]{1,0:T(8,128)(2,1)} %param.25), kind=kOutput, calls=%fused_computation.65 | convolution fusion | flops 50560640 | bytes 789504 | tf_op jit(solution)/shard_map/dot_general | solution.py:442
  69.3 1.7 %copy.130 = bf16[768,128]{1,0:T(8,128)(2,1)} copy(bf16[768,128]{0,1:T(8,128)(2,1)} %bitcast.186) | data formatting | bytes 393216 | tf_op jit(solution)/shard_map/dot_general | solution.py:441
  71.0 1.2 fusion.53
  72.2 1.0 pad_maximum_fusion
  73.3 2.6 %copy.133 = f32[256,4,256]{2,1,0:T(4,128)} copy(f32[256,4,256]{0,2,1:T(8,128)} %pad_maximum_fusion) | data formatting | bytes 2097152 | tf_op jit(solution)/shard_map/concatenate | solution.py:190
  75.8 2.7 %copy.134 = f32[4,2,4,8,2,2,256]{6,5,4,3,2,1,0:T(2,128)} copy(f32[4,2,4,8,2,2,256]{6,0,5,1,2,4,3:T(4,128)} %bitcast.174) | data formatting | bytes 2097152 | tf_op jit(solution)/shard_map/transpose | solution.py:191
  78.6 3.0 %reshape.610.ga = f32[4,256,256]{2,1,0:T(8,128)} reshape(f32[4,2,4,8,2,2,256]{6,5,4,3,2,1,0:T(2,128)} %copy.134) | data formatting | bytes 2097152 | tf_op jit(solution)/shard_map/reshape | solution.py:191
  81.7 1.2 copy-done.1
  82.9 45.4 %shard_map.170 = (f32[2,192]{1,0:T(2,128)S(1)}, f32[2,64]{1,0:T(2,128)S(1)}, f32[8,128]{1,0:T(8,128)S(1)}, f32[8,128]{1,0:T(8,128)S(1)}) custom-call(f32[4,256,256]{2,1,0:T(8,128)S(1)} %copy-done.1, f32[4,1024,128]{2,1,0:T(8,128)S(1)} %bitcast.172, f32[8,128]{1,0:T(8,128)S(1)} %maximum_bitcast_fusion.gs, bf16[128,128]{1,0:T(8,128)(2,1)S(1)} %copy-done.2), custom_call_target="tpu_custom_call" | custom-call | tf_op jit(solution)/shard_map/pallas_call | solution.py:196
  129.4 0.8 fusion.30
  130.2 0.6 copy.178
  131.3 0.6 copy.180
  (162 shorter events, 12.0 us)
Async XLA Ops:
  0.6 12.5 %copy-start = (bf16[1024,512]{1,0:T(8,128)(2,1)S(1)}, bf16[1024,512]{1,0:T(8,128)(2,1)}, u32[]{:S(2)}) copy-start(bf16[1024,512]{1,0:T(8,128)(2,1)} %param.28) | copy-start | bytes 3145732
  2.3 3.6 %copy-start.22 = (f32[4,32]{1,0:T(4,128)}, f32[4,32]{1,0:T(4,128)S(1)}, u32[]{:S(2)}) copy-start(f32[4,32]{1,0:T(4,128)S(1)} %get-tuple-element.175) | copy-start | bytes 1540
  4.4 1.3 copy-start.13
  4.7 0.9 copy-start.3
  5.0 7.7 %copy-start.27 = (f32[4]{0:T(128)S(1)}, f32[4]{0:T(128)}, u32[]{:S(2)}) copy-start(f32[4]{0:T(128)} %param.26) | copy-start | bytes 52
  5.0 8.2 %copy-start.24 = (pred[64,220]{1,0:T(32,128)(4,1)S(1)}, pred[64,220]{1,0:T(32,128)(4,1)}, u32[]{:S(2)}) copy-start(pred[64,220]{1,0:T(32,128)(4,1)} %constant.249.clone) | copy-start | bytes 42244
  5.0 8.2 %copy-start.21 = (bf16[2,16,512]{2,1,0:T(8,128)(2,1)S(1)}, bf16[2,16,512]{2,1,0:T(8,128)(2,1)}, u32[]{:S(2)}) copy-start(bf16[2,16,512]{2,1,0:T(8,128)(2,1)} %param.29) | copy-start | bytes 98308
  6.8 7.9 %copy-start.17 = (bf16[4,32,256]{2,1,0:T(8,128)(2,1)S(1)}, bf16[4,32,256]{2,1,0:T(8,128)(2,1)}, u32[]{:S(2)}) copy-start(bf16[4,32,256]{2,1,0:T(8,128)(2,1)} %param.30) | copy-start | bytes 196612
  6.8 7.9 %copy-start.15 = (bf16[256,256]{1,0:T(8,128)(2,1)S(1)}, bf16[256,256]{1,0:T(8,128)(2,1)}, u32[]{:S(2)}) copy-start(bf16[256,256]{1,0:T(8,128)(2,1)} %param.27) | copy-start | bytes 393220
  6.9 8.8 %collective-permute-start = (bf16[3,32,512]{2,1,0:T(8,128)(2,1)S(1)}, bf16[3,32,512]{2,1,0:T(8,128)(2,1)S(1)}, u32[]{:S(2)}, u32[]{:S(2)}) collective-permute-start(bf16[3,32,512]{2,1,0:T(8,128)(2,1)S(1)} %get-tuple-element.172), channel_id=1, source_target_pairs={{0,4},{4,8},{8,12},{12,16},{16,20},{20,24},{24,28},{28,32},{32,36}... | collective-permute-start | bytes 294920 | tf_op jit(solution)/shard_map/ppermute | solution.py:229
  8.9 6.7 %collective-permute-start.1 = (bf16[3,32,512]{2,1,0:T(8,128)(2,1)S(1)}, bf16[3,32,512]{2,1,0:T(8,128)(2,1)S(1)}, u32[]{:S(2)}, u32[]{:S(2)}) collective-permute-start(bf16[3,32,512]{2,1,0:T(8,128)(2,1)S(1)} %get-tuple-element.173), channel_id=1, source_target_pairs={{4,0},{8,4},{12,8},{16,12},{20,16},{24,20},{28,24},{32,28},{36,32}... | collective-permute-start | bytes 294920 | tf_op jit(solution)/shard_map/ppermute | solution.py:230
  13.8 11.7 %copy-start.8 = (f32[4,32,256]{2,1,0:T(8,128)}, f32[4,32,256]{2,1,0:T(8,128)S(1)}, u32[]{:S(2)}) copy-start(f32[4,32,256]{2,1,0:T(8,128)S(1)} %reshape.598) | copy-start | bytes 393220
  15.7 10.0 %collective-permute-start.3 = (bf16[10,3,512]{2,1,0:T(4,128)(2,1)S(1)}, bf16[10,3,512]{2,1,0:T(4,128)(2,1)S(1)}, u32[]{:S(2)}, u32[]{:S(2)}) collective-permute-start(bf16[10,3,512]{2,1,0:T(4,128)(2,1)S(1)} %get-tuple-element.170), channel_id=1, source_target_pairs={{1,0},{2,1},{3,2},{5,4},{6,5},{7,6},{9,8},{10,9},{11,10},{13,12},{... | collective-permute-start | bytes 92168 | tf_op jit(solution)/shard_map/ppermute | solution.py:230
  17.0 8.7 %collective-permute-start.2 = (bf16[10,3,512]{2,1,0:T(4,128)(2,1)S(1)}, bf16[10,3,512]{2,1,0:T(4,128)(2,1)S(1)}, u32[]{:S(2)}, u32[]{:S(2)}) collective-permute-start(bf16[10,3,512]{2,1,0:T(4,128)(2,1)S(1)} %get-tuple-element.171), channel_id=1, source_target_pairs={{0,1},{1,2},{2,3},{4,5},{5,6},{6,7},{8,9},{9,10},{10,11},{12,13},{... | collective-permute-start | bytes 92168 | tf_op jit(solution)/shard_map/ppermute | solution.py:229
  27.6 1.6 %copy-start.6 = (bf16[4,32,256]{2,1,0:T(8,128)(2,1)S(1)}, bf16[4,32,256]{2,1,0:T(8,128)(2,1)}, u32[]{:S(2)}) copy-start(bf16[4,32,256]{2,1,0:T(8,128)(2,1)} %param.23) | copy-start | bytes 196612
  29.3 1.9 %copy-start.16 = (bf16[4,32,256]{2,1,0:T(8,128)(2,1)}, bf16[4,32,256]{2,1,0:T(8,128)(2,1)S(1)}, u32[]{:S(2)}) copy-start(bf16[4,32,256]{2,1,0:T(8,128)(2,1)S(1)} %fusion.2) | copy-start | bytes 196612
  32.1 1.6 %copy-start.19 = (bf16[256,128]{1,0:T(8,128)(2,1)S(1)}, bf16[256,128]{1,0:T(8,128)(2,1)}, u32[]{:S(2)}) copy-start(bf16[256,128]{1,0:T(8,128)(2,1)} %copy.132) | copy-start | bytes 196612
  32.1 2.5 %copy-start.10 = (bf16[1024,32]{1,0:T(8,128)(2,1)S(1)}, bf16[1024,32]{1,0:T(8,128)(2,1)}, u32[]{:S(2)}) copy-start(bf16[1024,32]{1,0:T(8,128)(2,1)} %copy.135) | copy-start | bytes 196612
  32.1 2.4 %copy-start.20 = (bf16[4,128,32]{1,0,2:T(4,128)(2,1)S(1)}, bf16[4,128,32]{1,0,2:T(4,128)(2,1)}, u32[]{:S(2)}) copy-start(bf16[4,128,32]{1,0,2:T(4,128)(2,1)} %dot_general.111) | copy-start | bytes 98308
  32.4 13.4 %collective-permute-start.4 = (bf16[10,3,512]{2,1,0:T(4,128)(2,1)S(1)}, bf16[10,3,512]{2,1,0:T(4,128)(2,1)S(1)}, u32[]{:S(2)}, u32[]{:S(2)}) collective-permute-start(bf16[10,3,512]{2,1,0:T(4,128)(2,1)S(1)} %get-tuple-element.165), channel_id=1, source_target_pairs={{1,0},{2,1},{3,2},{5,4},{6,5},{7,6},{9,8},{10,9},{11,10},{13,12},{... | collective-permute-start | bytes 92168 | tf_op jit(solution)/shard_map/ppermute | solution.py:238
  34.6 1.8 %copy-start.11 = (f32[1,2,64,4,64]{2,4,3,1,0:T(8,128)S(1)}, f32[1,2,64,4,64]{2,4,3,1,0:T(8,128)}, u32[]{:S(2)}) copy-start(f32[1,2,64,4,64]{2,4,3,1,0:T(8,128)} %convolution_bitcast_fusion.1) | copy-start | bytes 393220
  36.8 13.7 %copy-start.14 = (f32[1,4,2,16,256]{4,3,2,1,0:T(8,128)S(1)}, f32[1,4,2,16,256]{4,3,2,1,0:T(8,128)}, u32[]{:S(2)}) copy-start(f32[1,4,2,16,256]{4,3,2,1,0:T(8,128)} %get-tuple-element.153) | copy-start | bytes 393220
  37.8 9.6 %collective-permute-start.5 = (bf16[10,3,512]{2,1,0:T(4,128)(2,1)S(1)}, bf16[10,3,512]{2,1,0:T(4,128)(2,1)S(1)}, u32[]{:S(2)}, u32[]{:S(2)}) collective-permute-start(bf16[10,3,512]{2,1,0:T(4,128)(2,1)S(1)} %get-tuple-element.164), channel_id=1, source_target_pairs={{0,1},{1,2},{2,3},{4,5},{5,6},{6,7},{8,9},{9,10},{10,11},{12,13},{... | collective-permute-start | bytes 92168 | tf_op jit(solution)/shard_map/ppermute | solution.py:238
  47.7 2.9 %copy-start.4 = (f32[10,32,512]{2,1,0:T(8,128)}, f32[10,32,512]{2,1,0:T(8,128)S(1)}, u32[]{:S(2)}) copy-start(f32[10,32,512]{2,1,0:T(8,128)S(1)} %scatter-add.27) | copy-start | bytes 1966084
  48.5 8.4 %collective-permute-start.6 = (bf16[3,32,512]{2,1,0:T(8,128)(2,1)}, bf16[3,32,512]{2,1,0:T(8,128)(2,1)}, u32[]{:S(2)}, u32[]{:S(2)}) collective-permute-start(bf16[3,32,512]{2,1,0:T(8,128)(2,1)} %get-tuple-element.167), channel_id=1, source_target_pairs={{4,0},{8,4},{12,8},{16,12},{20,16},{24,20},{28,24},{32,28},{36,32}... | collective-permute-start | bytes 294920 | tf_op jit(solution)/shard_map/ppermute | solution.py:238
  51.2 1.9 %copy-start.5 = (f32[10,32,512]{2,1,0:T(8,128)S(1)}, f32[10,32,512]{2,1,0:T(8,128)}, u32[]{:S(2)}) copy-start(f32[10,32,512]{2,1,0:T(8,128)} %copy-done.4) | copy-start | bytes 1966084
  53.2 5.9 %collective-permute-start.7 = (bf16[3,32,512]{2,1,0:T(8,128)(2,1)S(1)}, bf16[3,32,512]{2,1,0:T(8,128)(2,1)S(1)}, u32[]{:S(2)}, u32[]{:S(2)}) collective-permute-start(bf16[3,32,512]{2,1,0:T(8,128)(2,1)S(1)} %get-tuple-element.166), channel_id=1, source_target_pairs={{0,4},{4,8},{8,12},{12,16},{16,20},{20,24},{24,28},{28,32},{32,36}... | collective-permute-start | bytes 294920 | tf_op jit(solution)/shard_map/ppermute | solution.py:238
  67.8 4.5 %copy-start.12 = (f32[256,4,64]{0,2,1:T(8,128)S(1)}, f32[256,4,64]{0,2,1:T(8,128)}, u32[]{:S(2)}) copy-start(f32[256,4,64]{0,2,1:T(8,128)} %fusion.54) | copy-start | bytes 786436
  75.8 5.7 %copy-start.28 = (f32[4]{0:T(128)S(1)}, f32[4]{0:T(128)}, u32[]{:S(2)}) copy-start(f32[4]{0:T(128)} %reduce_sum.121) | copy-start | bytes 52
  75.8 5.8 %copy-start.2 = (bf16[128,128]{1,0:T(8,128)(2,1)S(1)}, bf16[128,128]{1,0:T(8,128)(2,1)}, u32[]{:S(2)}) copy-start(bf16[128,128]{1,0:T(8,128)(2,1)} %constant.250.clone.perm) | copy-start | bytes 98308
  78.6 50.8 %copy-start.7 = (bf16[4,32,256]{2,1,0:T(8,128)(2,1)S(1)}, bf16[4,32,256]{2,1,0:T(8,128)(2,1)}, u32[]{:S(2)}) copy-start(bf16[4,32,256]{2,1,0:T(8,128)(2,1)} %param.23) | copy-start | bytes 196612
  78.6 50.8 %copy-start.9 = (f32[4,32,256]{2,1,0:T(8,128)S(1)}, f32[4,32,256]{2,1,0:T(8,128)}, u32[]{:S(2)}) copy-start(f32[4,32,256]{2,1,0:T(8,128)} %copy-done.8) | copy-start | bytes 393220
  81.6 47.8 %copy-start.23 = (f32[4,32]{1,0:T(4,128)S(1)}, f32[4,32]{1,0:T(4,128)}, u32[]{:S(2)}) copy-start(f32[4,32]{1,0:T(4,128)} %copy-done.22) | copy-start | bytes 1540
  81.6 47.8 %copy-start.25 = (f32[256]{0:T(256)S(1)}, f32[256]{0:T(256)}, u32[]{:S(2)}) copy-start(f32[256]{0:T(256)} %param.24) | copy-start | bytes 3076
  81.6 47.8 %copy-start.26 = (f32[4,32]{1,0:T(4,128)S(1)}, f32[4,32]{1,0:T(4,128)}, u32[]{:S(2)}) copy-start(f32[4,32]{1,0:T(4,128)} %get-tuple-element.174) | copy-start | bytes 1540
  81.7 1.2 copy-start.1
  82.9 46.5 %copy-start.18 = (bf16[4,32,256]{2,1,0:T(8,128)(2,1)S(1)}, bf16[4,32,256]{2,1,0:T(8,128)(2,1)}, u32[]{:S(2)}) copy-start(bf16[4,32,256]{2,1,0:T(8,128)(2,1)} %param.30) | copy-start | bytes 196612

commit v2 on v1

v2 whole, which is shorter than its diff:
```python
import jax
import jax.numpy as jnp
import numpy as np
from jax import lax
from jax.experimental import pallas as pl
from jax.experimental.pallas import tpu as pltpu
from jax.sharding import PartitionSpec as P

EPS = 1e-06
MESH = pl.DeviceIdType.MESH
NX, NY, NZ = 4, 8, 8
ROWS, COLS = 128, 4
F32, BF16 = jnp.float32, jnp.bfloat16
OWN, SIDE, SLOT, NK = 128, 96, 16, 416
HALO = NK - OWN


def place():
    row, col = lax.axis_index("row"), lax.axis_index("col")
    return row // 16, (row // 8) % 2, (row // 2) % 4, row % 2, col


def device(y, zl, x, core, col):
    return (((y * 2 + zl) * 4 + x) * 2 + core, col)


def peers():
    y, zl, x, core, col = place()
    z = col * 2 + zl
    out = {"core": (core, [(1 - core, device(y, zl, x, 1 - core, col))])}
    out["x"] = (x, [])
    for p in range(1, NX):
        t = (x + p) % NX
        out["x"][1].append((t, device(y, zl, t, core, col)))
    out["y"] = (y, [])
    for p in range(1, NY):
        t = (y + p) % NY
        out["y"][1].append((t, device(t, zl, x, core, col)))
    out["z"] = (z, [])
    for p in range(1, NZ):
        t = (z + p) % NZ
        out["z"][1].append((t, device(y, t % 2, x, core, t // 2)))
    return out


def start_copies(copies):
    for c in copies:
        c.start()
    return copies


def wait_copies(copies):
    for c in copies:
        c.wait()


def exchange(peer_list, source, slots, send, recv):
    return start_copies(
        [
            pltpu.make_async_remote_copy(
                src_ref=source(t),
                dst_ref=slots.at[p],
                send_sem=send.at[p],
                recv_sem=recv.at[p],
                device_id=dev,
                device_id_type=MESH,
            )
            for p, (t, dev) in enumerate(peer_list)
        ]
    )


def spread(mine, peer_list, slots, send, recv):
    return start_copies(
        [
            pltpu.make_async_remote_copy(
                src_ref=slots.at[mine],
                dst_ref=slots.at[mine],
                send_sem=send.at[p],
                recv_sem=recv.at[p],
                device_id=dev,
                device_id_type=MESH,
            )
            for p, (t, dev) in enumerate(peer_list)
        ]
    )


def rows_at(ref, index, size):
    return ref.at[:, pl.ds(pl.multiple_of(index * size, size), size), :]


def token_list():
    return [(2 * i + pr, 2 * j + pc) for pr in range(2) for pc in range(2) for i in range(2) for j in range(16)]


def slot_tokens(first_row, rows, first_col):
    return [(first_row + i // 3, first_col + i % 3) for i in range(3 * rows)]


def one_hot(rows, width, where):
    out = np.zeros((rows, width), np.float32)
    for i, j in where:
        out[i, j] = 1
    return out


def tables():
    own = token_list()
    order = one_hot(128, 128, [(p, r * 32 + c) for p, (r, c) in enumerate(own)])
    sent = [(0, 4, 29), (0, 4, 0), (1, 3, 29), (1, 3, 0), (0, 3, 29), (0, 3, 0)]
    pick = one_hot(
        96, 128,
        [(16 * s + i, r * 32 + c) for s, a in enumerate(sent) for i, (r, c) in enumerate(slot_tokens(*a))],
    )
    every = np.concatenate([np.eye(128)[32:], np.eye(128)[:96], pick])
    back = order @ every.T
    key_at = np.full((NK, 2), 1000)
    key_at[:128] = own
    key_at[128:224] = [(k // 32 - 3, k % 32) for k in range(96)]
    key_at[224:320] = [(k // 32 + 4, k % 32) for k in range(96)]
    held = [(0, 4, -3), (0, 4, 32), (-3, 3, -3), (-3, 3, 32), (4, 3, -3), (4, 3, 32)]
    for s, a in enumerate(held):
        got = slot_tokens(*a)
        key_at[320 + 16 * s : 320 + 16 * s + len(got)] = got
    gap = np.abs(key_at[:, None, :] - np.asarray(own)[None, :, :])
    near = (gap <= 3).all(axis=-1).astype(np.float32)
    row_a = one_hot(
        256, 256,
        [((((k * 4 + x) * 8 + y) * 2 + zl) * 2 + j, ((y * 2 + zl) * 4 + x) * 4 + k * 2 + j)
         for k in range(2) for x in range(4) for y in range(8) for zl in range(2) for j in range(2)],
    )
    row_b = one_hot(
        256, 256,
        [((((k * 4 + x) * 2 + t) * 2 + zl) * 8 + j, t * 128 + zl * 64 + x * 16 + k * 8 + j)
         for k in range(2) for x in range(4) for t in range(2) for zl in range(2) for j in range(8)],
    )
    ones = np.kron(np.eye(4), np.ones((64, 64)))
    slab = one_hot(
        128, 128,
        [(y * 16 + c * 4 + k, c * 32 + y * 4 + k) for c in range(4) for y in range(8) for k in range(4)],
    )
    bf = lambda a: jnp.asarray(a, BF16)
    return (bf(order), bf(order.T), bf(pick), bf(back), jnp.asarray(near, F32), bf(row_a), bf(row_b), bf(ones), bf(np.eye(256)), bf(slab))


def nt(a, b):
    return lax.dot_general(a, b, (((1,), (1,)), ((), ())), preferred_element_type=F32)


def nn(a, b):
    return jnp.dot(a, b, preferred_element_type=F32)


def moved(table, value):
    return nn(table, value).astype(BF16)


def head_sums(value, ones):
    big = value.astype(BF16)
    small = (value - big.astype(F32)).astype(BF16)
    return nn(big, ones) + nn(small, ones)


def norm_rows(x, gain):
    inverse = lax.rsqrt(jnp.mean(x * x, axis=-1, keepdims=True) + EPS)
    return inverse, (x * inverse * gain).astype(BF16)


def body(tokens, gain, w_qkv, head_scale, w_out, w_merge, d_merged, d_skip,
         order, unorder, pick, back, near_mask, row_a, row_b, ones_t, eye, slab,
         o_skip, o_merged, o_tokens, o_qkv, o_out, o_merge, o_gain, o_scale,
         xk, strips, kv, kvt, st, pt, ptb, dst, q4, da4, keep, hs, hr, rhs, allowed,
         ga, ra1, sa2, ra2, sa3, ra3, sa4, ra4,
         gb, rb1, sb2, rb2, sb3, rb3, sb4, rb4,
         g1, g2, g3, g4, tsem_a, tsem_b, tsem_g, tsem_h):
    near = peers()
    core, x_at, y_at, z_at = (near[a][0] for a in ("core", "x", "y", "z"))
    row, col = lax.axis_index("row"), lax.axis_index("col")
    up, down = (row + ROWS - 1) % ROWS, (row + 1) % ROWS
    left, right = (col + COLS - 1) % COLS, (col + 1) % COLS
    toward = [(down, col), (up, col), (row, right), (row, left), (down, right), (down, left), (up, right), (up, left)]
    reverse = [(up, col), (down, col), (row, left), (row, right), (up, left), (up, right), (down, left), (down, right)]
    bar = pltpu.get_barrier_semaphore()
    for dev in toward:
        pl.semaphore_signal(bar, inc=1, device_id=dev, device_id_type=MESH)
    for axis in ("core", "x", "y", "z"):
        for _, dev in near[axis][1]:
            pl.semaphore_signal(bar, inc=1, device_id=dev, device_id_type=MESH)

    def sems(table, stage):
        return table.at[0, pl.ds(7 * stage, 7)], table.at[1, pl.ds(7 * stage, 7)]

    def halo(stage, devices, sources, targets):
        return start_copies([
            pltpu.make_async_remote_copy(
                src_ref=s, dst_ref=t, send_sem=tsem_h.at[0, 8 * stage + i], recv_sem=tsem_h.at[1, 8 * stage + i],
                device_id=dev, device_id_type=MESH)
            for i, (dev, s, t) in enumerate(zip(devices, sources, targets))
        ])

    strips[...] = moved(pick[...], tokens[...])
    pl.semaphore_wait(bar, 8 + 1 + 3 + 7 + 7)
    spans = [pl.ds(0, 96), pl.ds(96, 96)] + [pl.ds(192 + 16 * s, 16) for s in range(6)]
    ch = halo(
        0, toward,
        [tokens.at[pl.ds(32, 96)], tokens.at[pl.ds(0, 96)]] + [strips.at[pl.ds(16 * s, 16)] for s in range(6)],
        [xk.at[s] for s in spans],
    )

    ones = ones_t[...]
    gains = gain[...]
    lane = lax.broadcasted_iota(jnp.int32, (1, 256), 1) // 64
    scales = jnp.zeros((1, 256), F32)
    for h in range(4):
        scales = jnp.where(lane == h, head_scale[h], scales)
    xp = moved(order[...], tokens[...])
    x = xp.astype(F32)
    inverse, normed = norm_rows(x, gains)
    qkv = nn(normed, w_qkv[...])
    q, k = qkv[:, :256], qkv[:, 256:512]
    q_norm = lax.rsqrt(head_sums(q * q, ones) + EPS)
    k_norm = lax.rsqrt(head_sums(k * k, ones) + EPS)
    q_unit, k_unit = q * q_norm, k * k_norm
    q_hat = (q_unit * scales).astype(BF16)
    keep[0], keep[1], keep[2], keep[3] = q_norm, k_norm, q_unit, k_unit
    kv[:OWN, :256] = k_unit.astype(BF16)
    kv[:OWN, 256:] = qkv[:, 512:].astype(BF16)
    zero = jnp.zeros((), BF16)
    for h in range(4):
        q4[128 * h : 128 * h + 128] = jnp.where(lane == h, q_hat, zero)

    d_group = nt(d_merged[...], w_merge[...])
    d_y = moved(order[...], d_skip[...]).astype(F32) + jnp.concatenate(
        [d_group[:, 256 * g : 256 * g + 256] for g in range(4)], axis=0)
    dy_b = d_y.astype(BF16)
    keep[4] = d_y
    d_attn = nt(dy_b, w_out[...]).astype(BF16)
    for h in range(4):
        da4[128 * h : 128 * h + 128] = jnp.where(lane == h, d_attn, zero)

    yes = lambda c: jnp.where(c, 1.0, 0.0).astype(F32)
    v_up, v_down, v_left, v_right = yes(row > 0), yes(row < ROWS - 1), yes(col > 0), yes(col < COLS - 1)
    factors = [(128, 96, v_up), (224, 96, v_down), (320, 16, v_left), (336, 16, v_right),
               (352, 16, v_up * v_left), (368, 16, v_up * v_right), (384, 16, v_down * v_left), (400, 16, v_down * v_right)]
    allowed[:OWN] = near_mask[:OWN]
    for at, size, f in factors:
        allowed[at : at + size] = near_mask[at : at + size] * f

    wait_copies(ch)
    _, normed_h = norm_rows(xk[...].astype(F32), gains)
    kv_h = nn(normed_h, w_qkv[:, 256:])
    k_h = kv_h[:, :256]
    kv[OWN:, :256] = (k_h * lax.rsqrt(head_sums(k_h * k_h, ones) + EPS)).astype(BF16)
    kv[OWN:, 256:] = kv_h[:, 256:].astype(BF16)

    st[...] = nt(kv[:, :256], q4[...])
    for h in range(4):
        span = slice(128 * h, 128 * h + 128)
        e = jnp.exp(st[:, span]) * allowed[...]
        p = e * (1.0 / jnp.sum(e, axis=0, keepdims=True))
        pt[:, span] = p
        ptb[:, span] = p.astype(BF16)
    kvt[:256] = nt(eye[...], kv[:, :256]).astype(BF16)
    kvt[256:] = nt(eye[...], kv[:, 256:]).astype(BF16)

    def diagonal(full):
        return jnp.concatenate([full[64 * h : 64 * h + 64, 128 * h : 128 * h + 128] for h in range(4)], axis=0).T

    attn = diagonal(nn(kvt[256:], ptb[...])).astype(BF16)
    skip = (x + nn(attn, w_out[...])).astype(BF16)
    dm = d_merged[...]
    for g in range(4):
        part = nn(nt(row_b[...], skip[32 * g : 32 * g + 32]).astype(BF16), dm)
        for c in range(4):
            gb[c, g] = part[:, 128 * c : 128 * c + 128].astype(BF16)
    mine = lambda size, index: pl.ds(pl.multiple_of(index * size, size), size)
    cb = exchange(near["core"][1], lambda t: gb.at[:, :, mine(128, t), :], rb1, *sems(tsem_b, 0))
    o_skip[...] = moved(unorder[...], skip)
    group = jnp.concatenate([skip[32 * g : 32 * g + 32] for g in range(4)], axis=1)
    o_merged[...] = nn(group, w_merge[...]).astype(BF16)

    st[...] = nt(kv[:, 256:], da4[...])
    for h in range(4):
        span = slice(128 * h, 128 * h + 128)
        dw, p = st[:, span], pt[:, span]
        dst[:, span] = (p * (dw - jnp.sum(dw * p, axis=0, keepdims=True))).astype(BF16)
    hs[:, :256] = nn(dst[OWN:], q4[...]).astype(BF16)
    hs[:, 256:] = nn(ptb[OWN:], da4[...]).astype(BF16)
    ch = halo(1, reverse, [hs.at[s] for s in spans], [hr.at[s] for s in spans])

    wait_copies(cb)
    sb2[...] = (gb[:, :, mine(128, core), :].astype(F32) + rb1[0].astype(F32)).astype(BF16)
    cb = exchange(near["x"][1], lambda t: sb2.at[:, :, mine(32, t), :], rb2, *sems(tsem_b, 1))

    d_k = nn(dst[:OWN], q4[...])
    d_v = nn(ptb[:OWN], da4[...])
    d_qhat = diagonal(nn(kvt[:256], dst[...]))
    u = keep[2]
    scale_row = jnp.sum(u * d_qhat, axis=0, keepdims=True)
    g_u = d_qhat * scales
    d_q = (keep[0] * (g_u - u * head_sums(u * g_u, ones))).astype(BF16)
    lhs = jnp.concatenate([nt(row_a[...], normed), nt(row_a[...], attn)], axis=1).astype(BF16)
    rhs[...] = jnp.zeros_like(rhs)
    dy_b = keep[4].astype(BF16)
    for c in range(4):
        rhs[128:, 256 * c + 192 : 256 * c + 256] = dy_b[:, 64 * c : 64 * c + 64]

    wait_copies(ch)
    added = nn(back[...], hr[...])
    d_k = d_k + added[:, :256]
    d_v = d_v + added[:, 256:]
    ku = keep[3]
    d_kraw = (keep[1] * (d_k - ku * head_sums(ku * d_k, ones))).astype(BF16)
    d_qkv = jnp.concatenate([d_q, d_kraw, d_v.astype(BF16)], axis=1)
    for c in range(4):
        rhs[:128, 256 * c : 256 * c + 192] = d_qkv[:, 192 * c : 192 * c + 192]
    for c in range(4):
        ga[c] = nn(lhs, rhs[:, 256 * c : 256 * c + 256]).astype(BF16)
    ca = exchange(near["core"][1], lambda t: rows_at(ga, t, 128), ra1, *sems(tsem_a, 0))

    d_normed = nt(d_qkv, w_qkv[...])
    x = xp.astype(F32)
    gain_row = jnp.sum(x * inverse * d_normed, axis=0, keepdims=True)
    for i, r in enumerate((gain_row[:, :128], gain_row[:, 128:], scale_row[:, :128], scale_row[:, 128:])):
        g1[core, i : i + 1] = r
    g1[core, 4:8] = jnp.zeros((4, 128), F32)
    cg = spread(core, near["core"][1], g1, *sems(tsem_g, 0))

    scaled = gains * d_normed
    g_x = inverse * scaled - x * (inverse * inverse * inverse) * jnp.mean(x * scaled, axis=-1, keepdims=True)
    o_tokens[...] = moved(unorder[...], (keep[4] + g_x).astype(BF16))

    wait_copies(ca)
    sa2[...] = (ga[:, mine(128, core), :].astype(F32) + ra1[0].astype(F32)).astype(BF16)
    ca = exchange(near["x"][1], lambda t: rows_at(sa2, t, 32), ra2, *sems(tsem_a, 1))
    wait_copies(cg)
    g2[x_at] = g1[0] + g1[1]
    cg = spread(x_at, near["x"][1], g2, *sems(tsem_g, 1))
    wait_copies(cb)
    total = sb2[:, :, mine(32, x_at), :].astype(F32)
    for p in range(3):
        total = total + rb2[p].astype(F32)
    sb3[...] = total.astype(BF16)
    cb = exchange(near["y"][1], lambda t: sb3.at[:, t // 2, mine(16, t % 2), :], rb3, *sems(tsem_b, 2))

    wait_copies(ca)
    total = sa2[:, mine(32, x_at), :].astype(F32)
    for p in range(3):
        total = total + ra2[p].astype(F32)
    sa3[...] = moved(slab[...], total.astype(BF16).reshape(128, 256)).reshape(8, 16, 256)
    ca = exchange(near["y"][1], lambda t: sa3.at[t], ra3, *sems(tsem_a, 2))
    wait_copies(cg)
    g3[y_at] = (g2[0] + g2[1]) + (g2[2] + g2[3])
    cg = spread(y_at, near["y"][1], g3, *sems(tsem_g, 2))
    wait_copies(cb)
    total = sb3[:, y_at // 2, mine(16, y_at % 2), :].astype(F32)
    for p in range(7):
        total = total + rb3[p].astype(F32)
    sb4[...] = total
    cb = exchange(near["z"][1], lambda t: sb4.at[t // 2, mine(8, t % 2), :], rb4, *sems(tsem_b, 3))

    wait_copies(ca)
    total = sa3[y_at].astype(F32)
    for p in range(7):
        total = total + ra3[p].astype(F32)
    sa4[...] = total.reshape(2, 8, 256)
    ca = exchange(near["z"][1], lambda t: sa4.at[t // 4], ra4, *sems(tsem_a, 3))
    wait_copies(cg)
    g4[z_at] = ((g3[0] + g3[1]) + (g3[2] + g3[3])) + ((g3[4] + g3[5]) + (g3[6] + g3[7]))
    cg = spread(z_at, near["z"][1], g4, *sems(tsem_g, 3))
    wait_copies(cb)
    total = sb4[z_at // 2, mine(8, z_at % 2), :]
    for p in range(7):
        total = total + rb4[p]
    o_merge[...] = total

    wait_copies(ca)
    total = sa4[z_at // 4]
    for p in range(7):
        total = total + ra4[p]
    part = z_at % 4
    piece = jnp.zeros((2, 256), F32)
    for i in range(4):
        piece = piece + jnp.where(part == i, total[2 * i : 2 * i + 2], 0.0)
    o_qkv[...] = piece[:, :192]
    o_out[...] = piece[:, 192:]
    wait_copies(cg)
    total = ((g4[0] + g4[1]) + (g4[2] + g4[3])) + ((g4[4] + g4[5]) + (g4[6] + g4[7]))
    o_gain[...] = total[0:2]
    halves = lax.broadcasted_iota(jnp.int32, (1, 128), 1)
    out = jnp.zeros((1, 128), F32)
    for h in range(4):
        r = total[2 + h // 2 : 3 + h // 2]
        s = jnp.sum(jnp.where(halves // 64 == h % 2, r, 0.0), axis=1, keepdims=True)
        out = jnp.where(halves == h, s, out)
    o_scale[...] = out


def on_device(tokens, gain, w_qkv, head_scale, w_out, w_merge, d_merged, d_skip):
    V = pltpu.VMEM
    S = jax.ShapeDtypeStruct
    vmem = pl.BlockSpec(memory_space=V)
    smem = pl.BlockSpec(memory_space=pltpu.SMEM)
    DMA = pltpu.SemaphoreType.DMA
    out = pl.pallas_call(
        body,
        out_shape=(
            S((128, 256), BF16), S((32, 512), BF16), S((128, 256), BF16),
            S((2, 192), F32), S((2, 64), F32), S((8, 128), F32), S((2, 128), F32), S((1, 128), F32),
        ),
        in_specs=[vmem] * 3 + [smem] + [vmem] * 14,
        out_specs=(vmem,) * 8,
        scratch_shapes=[
            V((HALO, 256), BF16), V((96, 256), BF16), V((NK, 512), BF16), V((512, NK), BF16),
            V((NK, 512), F32), V((NK, 512), F32), V((NK, 512), BF16), V((NK, 512), BF16),
            V((512, 256), BF16), V((512, 256), BF16), V((5, 128, 256), F32),
            V((HALO, 512), BF16), V((HALO, 512), BF16), V((256, 1024), BF16), V((NK, 128), F32),
            V((4, 256, 256), BF16), V((1, 4, 128, 256), BF16),
            V((4, 128, 256), BF16), V((3, 4, 32, 256), BF16),
            V((8, 16, 256), BF16), V((7, 16, 256), BF16),
            V((2, 8, 256), F32), V((7, 8, 256), F32),
            V((4, 4, 256, 128), BF16), V((1, 4, 4, 128, 128), BF16),
            V((4, 4, 128, 128), BF16), V((3, 4, 4, 32, 128), BF16),
            V((4, 4, 32, 128), BF16), V((7, 4, 16, 128), BF16),
            V((4, 16, 128), F32), V((7, 8, 128), F32),
            V((2, 8, 128), F32), V((4, 8, 128), F32), V((8, 8, 128), F32), V((8, 8, 128), F32),
            DMA((2, 28)), DMA((2, 28)), DMA((2, 28)), DMA((2, 16)),
        ],
        compiler_params=pltpu.CompilerParams(collective_id=0, has_side_effects=True, vmem_limit_bytes=48 * 2**20),
    )(
        tokens.reshape(128, 256), gain.reshape(1, 256), w_qkv, head_scale, w_out, w_merge,
        d_merged.reshape(32, 512), d_skip.reshape(128, 256), *tables(),
    )
    skip, merged, grad, qkv, o, m, g, s = out
    return (skip.reshape(4, 32, 256), merged.reshape(2, 16, 512), grad.reshape(4, 32, 256), qkv, o, m, g.reshape(256), s[0, :4])


def solution(mesh):
    return jax.shard_map(
        on_device,
        mesh=mesh,
        in_specs=(
            P("row", "col", None),
            P(),
            P(),
            P(),
            P(),
            P(),
            P("row", "col", None),
            P("row", "col", None),
        ),
        out_specs=(
            P("row", "col", None),
            P("row", "col", None),
            P("row", "col", None),
            P("row", "col"),
            P("row", "col"),
            P("row", "col"),
            P(),
            P(),
        ),
        check_vma=False,
    )
```

time: 135 us -> 70.5 us (0.52); the launches traced: 132 us -> 69.7 us
  starting transfers between devices: 28.6 us -> 0 us
  local copies, waits for them, and re-layouts: 33 us -> 19.4 us
  other arithmetic: 11.1 us -> 0 us
  matrix products: 9.61 us -> 0 us
  Pallas kernels: 45.4 us -> 49.7 us
  waiting for transfers between devices: 2.49 us -> 0 us
    ppermute x8 -> x0, starting transfers between devices: 28.6 us -> none  [the longest x4 14.9 us: passed_along(): lax.ppermute(value, axis, [(source, source + steps) for source in range(i...]
    unnamed x66 -> x43, local copies, waits for them, and re-layouts: 5.08 us -> 18.8 us
    dot_general x14 -> x0, matrix products: 9.24 us -> none  [the longest x1 1.73 us: on_device(): jnp.dot(merge_in.T, flat_dm, preferred_element_type=jnp.float32)]
    reshape x11 -> x0, local copies, waits for them, and re-layouts: 5.46 us -> none  [the longest x1 2.98 us: reduce_all(): a.reshape(8, 2, 4, 2, 2, 4, 256).transpose(5, 3, 2, 0, 1, 4, 6)]
    transpose x6 -> x0, local copies, waits for them, and re-layouts: 4.92 us -> none  [the longest x1 2.75 us: reduce_all(): a.reshape(8, 2, 4, 2, 2, 4, 256).transpose(5, 3, 2, 0, 1, 4, 6)]
    pallas_call x1, Pallas kernels: 45.4 us -> 49.7 us  [on_device(): pl.pallas_call(body, out_shape=(S((128, 256), BF16), S((32, 512), BF16),...]
    dot_general x4 -> x0, local copies, waits for them, and re-layouts: 3.91 us -> none  [the longest x1 1.74 us: on_device(): grad_qkv = jnp.dot(flat_normed.T, d_qkv, preferred_element_type=jnp.float32)]
    reduce_sum x5 -> x0, other arithmetic: 3.52 us -> none  [the longest x1 1.61 us: on_device(): jnp.sum(q_unit * g_unit, axis=-1, keepdims=True)]
  transfers between devices with their start and end apart: 8 -> 0, of which waited for: 2 -> 0; matrix products, arithmetic and copies ran while one was open for 10% -> 0% of each run, Pallas kernels for 0% -> 0%
where the time goes in v2:
time: 70.5 us; the launch traced here: 69.7 us
  Pallas kernels  49.7 us (70%)
  local copies, waits for them, and re-layouts  19.4 us (28%)
    pallas_call x1, Pallas kernels, on_device(): pl.pallas_call(body, out_shape=(S((128, 256), BF16), S((32, 512), BF16),...  49.7 us
    unnamed x43, local copies, waits for them, and re-layouts  18.8 us

profile of v2, /device:TPU:6, one launch (start us, length us, event | category | flops | bytes accessed | tf_op | source)
XLA Modules:
  0.0 69.7 jit_solution(17360354888144999504)
XLA Ops:
  0.6 0.0 copy-start.16
  0.6 0.0 copy-start.17
  0.7 0.7 copy-done.16
  1.3 0.0 copy-done.17
  1.3 0.0 copy-start
  1.3 1.2 %copy-done = bf16[1024,512]{1,0:T(8,128)(2,1)S(1)} copy-done((bf16[1024,512]{1,0:T(8,128)(2,1)S(1)}, bf16[1024,512]{1,0:T(8,128)(2,1)}, u32[]{:S(2)}) %copy-start) | copy-done | bytes 1048600
  2.5 0.0 copy-start.1
  2.5 1.0 %copy-done.1 = bf16[256,768]{1,0:T(8,128)(2,1)S(1)} copy-done((bf16[256,768]{1,0:T(8,128)(2,1)S(1)}, bf16[256,768]{1,0:T(8,128)(2,1)}, u32[]{:S(2)}) %copy-start.1) | copy-done | bytes 393240
  3.5 0.0 copy-start.2
  3.5 0.9 %copy-done.2 = f32[416,128]{1,0:T(8,128)S(1)} copy-done((f32[416,128]{1,0:T(8,128)S(1)}, f32[416,128]{1,0:T(8,128)}, u32[]{:S(2)}) %copy-start.2) | copy-done | bytes 213016
  4.5 0.0 copy-start.3
  4.5 0.9 %copy-done.3 = bf16[256,256]{1,0:T(8,128)(2,1)S(1)} copy-done((bf16[256,256]{1,0:T(8,128)(2,1)S(1)}, bf16[256,256]{1,0:T(8,128)(2,1)}, u32[]{:S(2)}) %copy-start.3) | copy-done | bytes 131096
  5.4 0.0 copy-start.4
  5.4 0.9 %copy-done.4 = bf16[256,256]{1,0:T(8,128)(2,1)S(1)} copy-done((bf16[256,256]{1,0:T(8,128)(2,1)S(1)}, bf16[256,256]{1,0:T(8,128)(2,1)}, u32[]{:S(2)}) %copy-start.4) | copy-done | bytes 131096
  6.3 0.0 copy-start.5
  6.3 0.9 %copy-done.5 = bf16[256,256]{1,0:T(8,128)(2,1)S(1)} copy-done((bf16[256,256]{1,0:T(8,128)(2,1)S(1)}, bf16[256,256]{1,0:T(8,128)(2,1)}, u32[]{:S(2)}) %copy-start.5) | copy-done | bytes 131096
  7.2 0.0 copy-start.6
  7.2 0.9 %copy-done.6 = bf16[256,256]{1,0:T(8,128)(2,1)S(1)} copy-done((bf16[256,256]{1,0:T(8,128)(2,1)S(1)}, bf16[256,256]{1,0:T(8,128)(2,1)}, u32[]{:S(2)}) %copy-start.6) | copy-done | bytes 131096
  8.1 0.0 copy-start.7
  8.1 0.9 %copy-done.7 = bf16[256,256]{1,0:T(8,128)(2,1)S(1)} copy-done((bf16[256,256]{1,0:T(8,128)(2,1)S(1)}, bf16[256,256]{1,0:T(8,128)(2,1)}, u32[]{:S(2)}) %copy-start.7) | copy-done | bytes 131096
  9.0 0.0 copy-start.8
  9.0 0.9 %copy-done.8 = bf16[128,288]{1,0:T(8,128)(2,1)S(1)} copy-done((bf16[128,288]{1,0:T(8,128)(2,1)S(1)}, bf16[128,288]{1,0:T(8,128)(2,1)}, u32[]{:S(2)}) %copy-start.8) | copy-done | bytes 73752
  9.9 0.0 copy-start.9
  9.9 0.8 %copy-done.9 = bf16[4,32,256]{2,1,0:T(8,128)(2,1)S(1)} copy-done((bf16[4,32,256]{2,1,0:T(8,128)(2,1)S(1)}, bf16[4,32,256]{2,1,0:T(8,128)(2,1)}, u32[]{:S(2)}) %copy-start.9) | copy-done | bytes 65560
  10.7 0.0 copy-start.10
  10.7 0.8 %copy-done.10 = bf16[4,32,256]{2,1,0:T(8,128)(2,1)S(1)} copy-done((bf16[4,32,256]{2,1,0:T(8,128)(2,1)S(1)}, bf16[4,32,256]{2,1,0:T(8,128)(2,1)}, u32[]{:S(2)}) %copy-start.10) | copy-done | bytes 65560
  11.6 0.0 copy-start.11
  11.6 0.8 %copy-done.11 = bf16[2,16,512]{2,1,0:T(8,128)(2,1)S(1)} copy-done((bf16[2,16,512]{2,1,0:T(8,128)(2,1)S(1)}, bf16[2,16,512]{2,1,0:T(8,128)(2,1)}, u32[]{:S(2)}) %copy-start.11) | copy-done | bytes 32792
  12.3 0.0 copy-start.12
  12.3 0.8 %copy-done.12 = bf16[128,128]{1,0:T(8,128)(2,1)S(1)} copy-done((bf16[128,128]{1,0:T(8,128)(2,1)S(1)}, bf16[128,128]{1,0:T(8,128)(2,1)}, u32[]{:S(2)}) %copy-start.12) | copy-done | bytes 32792
  13.1 0.0 copy-start.13
  13.1 0.8 %copy-done.13 = bf16[128,128]{1,0:T(8,128)(2,1)S(1)} copy-done((bf16[128,128]{1,0:T(8,128)(2,1)S(1)}, bf16[128,128]{1,0:T(8,128)(2,1)}, u32[]{:S(2)}) %copy-start.13) | copy-done | bytes 32792
  13.8 0.0 copy-start.14
  13.8 0.8 %copy-done.14 = bf16[128,128]{1,0:T(8,128)(2,1)S(1)} copy-done((bf16[128,128]{1,0:T(8,128)(2,1)S(1)}, bf16[128,128]{1,0:T(8,128)(2,1)}, u32[]{:S(2)}) %copy-start.14) | copy-done | bytes 32792
  14.6 0.0 copy-start.15
  14.6 0.7 %copy-done.15 = bf16[96,128]{1,0:T(8,128)(2,1)S(1)} copy-done((bf16[96,128]{1,0:T(8,128)(2,1)S(1)}, bf16[96,128]{1,0:T(8,128)(2,1)}, u32[]{:S(2)}) %copy-start.15) | copy-done | bytes 24600
  15.3 49.7 %shard_map.233 = (bf16[128,256]{1,0:T(8,128)(2,1)S(1)}, bf16[32,512]{1,0:T(8,128)(2,1)S(1)}, bf16[128,256]{1,0:T(8,128)(2,1)S(1)}, f32[2,192]{1,0:T(2,128)S(1)},...) custom-call(bf16[128,256]{1,0:T(8,128)(2,1)S(1)} %bitcast.10, ...), custom_call_target="tpu_custom_call" | custom-call | tf_op jit(solution)/shard_map/pallas_call | solution.py:406
  65.0 0.5 slice_bitcast_fusion
  65.5 0.6 copy.33
  66.2 0.6 copy.34
  66.8 0.6 copy.35
  67.4 0.6 copy.36
  68.0 0.6 copy.37
  68.5 0.6 copy.38
  69.1 0.6 copy.39
Async XLA Ops:
  0.6 0.7 copy-start.16
  0.6 0.7 copy-start.17
  1.3 1.2 %copy-start = (bf16[1024,512]{1,0:T(8,128)(2,1)S(1)}, bf16[1024,512]{1,0:T(8,128)(2,1)}, u32[]{:S(2)}) copy-start(bf16[1024,512]{1,0:T(8,128)(2,1)} %w_merge.1) | copy-start | bytes 3145732
  2.5 1.0 %copy-start.1 = (bf16[256,768]{1,0:T(8,128)(2,1)S(1)}, bf16[256,768]{1,0:T(8,128)(2,1)}, u32[]{:S(2)}) copy-start(bf16[256,768]{1,0:T(8,128)(2,1)} %w_qkv.1) | copy-start | bytes 1179652
  3.5 0.9 %copy-start.2 = (f32[416,128]{1,0:T(8,128)S(1)}, f32[416,128]{1,0:T(8,128)}, u32[]{:S(2)}) copy-start(f32[416,128]{1,0:T(8,128)} %constant.24.clone.near_mask) | copy-start | bytes 638980
  4.5 0.9 %copy-start.3 = (bf16[256,256]{1,0:T(8,128)(2,1)S(1)}, bf16[256,256]{1,0:T(8,128)(2,1)}, u32[]{:S(2)}) copy-start(bf16[256,256]{1,0:T(8,128)(2,1)} %w_out.1) | copy-start | bytes 393220
  5.4 0.9 %copy-start.4 = (bf16[256,256]{1,0:T(8,128)(2,1)S(1)}, bf16[256,256]{1,0:T(8,128)(2,1)}, u32[]{:S(2)}) copy-start(bf16[256,256]{1,0:T(8,128)(2,1)} %constant.28.clone.eye) | copy-start | bytes 393220
  6.3 0.9 %copy-start.5 = (bf16[256,256]{1,0:T(8,128)(2,1)S(1)}, bf16[256,256]{1,0:T(8,128)(2,1)}, u32[]{:S(2)}) copy-start(bf16[256,256]{1,0:T(8,128)(2,1)} %constant.27.clone.ones_t) | copy-start | bytes 393220
  7.2 0.9 %copy-start.6 = (bf16[256,256]{1,0:T(8,128)(2,1)S(1)}, bf16[256,256]{1,0:T(8,128)(2,1)}, u32[]{:S(2)}) copy-start(bf16[256,256]{1,0:T(8,128)(2,1)} %constant.26.clone.row_b) | copy-start | bytes 393220
  8.1 0.9 %copy-start.7 = (bf16[256,256]{1,0:T(8,128)(2,1)S(1)}, bf16[256,256]{1,0:T(8,128)(2,1)}, u32[]{:S(2)}) copy-start(bf16[256,256]{1,0:T(8,128)(2,1)} %constant.25.clone.row_a) | copy-start | bytes 393220
  9.0 0.9 %copy-start.8 = (bf16[128,288]{1,0:T(8,128)(2,1)S(1)}, bf16[128,288]{1,0:T(8,128)(2,1)}, u32[]{:S(2)}) copy-start(bf16[128,288]{1,0:T(8,128)(2,1)} %constant.23.clone.back) | copy-start | bytes 221188
  9.9 0.8 %copy-start.9 = (bf16[4,32,256]{2,1,0:T(8,128)(2,1)S(1)}, bf16[4,32,256]{2,1,0:T(8,128)(2,1)}, u32[]{:S(2)}) copy-start(bf16[4,32,256]{2,1,0:T(8,128)(2,1)} %param.18) | copy-start | bytes 196612
  10.7 0.8 %copy-start.10 = (bf16[4,32,256]{2,1,0:T(8,128)(2,1)S(1)}, bf16[4,32,256]{2,1,0:T(8,128)(2,1)}, u32[]{:S(2)}) copy-start(bf16[4,32,256]{2,1,0:T(8,128)(2,1)} %param.25) | copy-start | bytes 196612
  11.6 0.8 %copy-start.11 = (bf16[2,16,512]{2,1,0:T(8,128)(2,1)S(1)}, bf16[2,16,512]{2,1,0:T(8,128)(2,1)}, u32[]{:S(2)}) copy-start(bf16[2,16,512]{2,1,0:T(8,128)(2,1)} %param.24) | copy-start | bytes 98308
  12.3 0.8 %copy-start.12 = (bf16[128,128]{1,0:T(8,128)(2,1)S(1)}, bf16[128,128]{1,0:T(8,128)(2,1)}, u32[]{:S(2)}) copy-start(bf16[128,128]{1,0:T(8,128)(2,1)} %constant.29.clone.slab) | copy-start | bytes 98308
  13.1 0.8 %copy-start.13 = (bf16[128,128]{1,0:T(8,128)(2,1)S(1)}, bf16[128,128]{1,0:T(8,128)(2,1)}, u32[]{:S(2)}) copy-start(bf16[128,128]{1,0:T(8,128)(2,1)} %constant.21.clone.unorder) | copy-start | bytes 98308
  13.8 0.8 %copy-start.14 = (bf16[128,128]{1,0:T(8,128)(2,1)S(1)}, bf16[128,128]{1,0:T(8,128)(2,1)}, u32[]{:S(2)}) copy-start(bf16[128,128]{1,0:T(8,128)(2,1)} %constant.20.clone.order) | copy-start | bytes 98308
  14.6 0.7 %copy-start.15 = (bf16[96,128]{1,0:T(8,128)(2,1)S(1)}, bf16[96,128]{1,0:T(8,128)(2,1)}, u32[]{:S(2)}) copy-start(bf16[96,128]{1,0:T(8,128)(2,1)} %constant.22.clone.pick) | copy-start | bytes 73732

commit v3 on v2

--- a/solution.py
+++ b/solution.py
@@ -1,6 +1,5 @@
 import jax
 import jax.numpy as jnp
-import numpy as np
 from jax import lax
 from jax.experimental import pallas as pl
 from jax.experimental.pallas import tpu as pltpu
@@ -11,7 +10,8 @@
 NX, NY, NZ = 4, 8, 8
 ROWS, COLS = 128, 4
 F32, BF16 = jnp.float32, jnp.bfloat16
-OWN, SIDE, SLOT, NK = 128, 96, 16, 416
+OWN, NK = 128, 416
+VMEM_LIMIT = 63 * 2**20
 HALO = NK - OWN
 
 
@@ -90,58 +90,65 @@
     return ref.at[:, pl.ds(pl.multiple_of(index * size, size), size), :]
 
 
-def token_list():
-    return [(2 * i + pr, 2 * j + pc) for pr in range(2) for pc in range(2) for i in range(2) for j in range(16)]
-
-
-def slot_tokens(first_row, rows, first_col):
-    return [(first_row + i // 3, first_col + i % 3) for i in range(3 * rows)]
-
-
-def one_hot(rows, width, where):
-    out = np.zeros((rows, width), np.float32)
-    for i, j in where:
-        out[i, j] = 1
-    return out
-
-
-def tables():
-    own = token_list()
-    order = one_hot(128, 128, [(p, r * 32 + c) for p, (r, c) in enumerate(own)])
-    sent = [(0, 4, 29), (0, 4, 0), (1, 3, 29), (1, 3, 0), (0, 3, 29), (0, 3, 0)]
-    pick = one_hot(
-        96, 128,
-        [(16 * s + i, r * 32 + c) for s, a in enumerate(sent) for i, (r, c) in enumerate(slot_tokens(*a))],
-    )
-    every = np.concatenate([np.eye(128)[32:], np.eye(128)[:96], pick])
-    back = order @ every.T
-    key_at = np.full((NK, 2), 1000)
-    key_at[:128] = own
-    key_at[128:224] = [(k // 32 - 3, k % 32) for k in range(96)]
-    key_at[224:320] = [(k // 32 + 4, k % 32) for k in range(96)]
-    held = [(0, 4, -3), (0, 4, 32), (-3, 3, -3), (-3, 3, 32), (4, 3, -3), (4, 3, 32)]
-    for s, a in enumerate(held):
-        got = slot_tokens(*a)
-        key_at[320 + 16 * s : 320 + 16 * s + len(got)] = got
-    gap = np.abs(key_at[:, None, :] - np.asarray(own)[None, :, :])
-    near = (gap <= 3).all(axis=-1).astype(np.float32)
-    row_a = one_hot(
-        256, 256,
-        [((((k * 4 + x) * 8 + y) * 2 + zl) * 2 + j, ((y * 2 + zl) * 4 + x) * 4 + k * 2 + j)
-         for k in range(2) for x in range(4) for y in range(8) for zl in range(2) for j in range(2)],
-    )
-    row_b = one_hot(
-        256, 256,
-        [((((k * 4 + x) * 2 + t) * 2 + zl) * 8 + j, t * 128 + zl * 64 + x * 16 + k * 8 + j)
-         for k in range(2) for x in range(4) for t in range(2) for zl in range(2) for j in range(8)],
-    )
-    ones = np.kron(np.eye(4), np.ones((64, 64)))
-    slab = one_hot(
-        128, 128,
-        [(y * 16 + c * 4 + k, c * 32 + y * 4 + k) for c in range(4) for y in range(8) for k in range(4)],
-    )
-    bf = lambda a: jnp.asarray(a, BF16)
-    return (bf(order), bf(order.T), bf(pick), bf(back), jnp.asarray(near, F32), bf(row_a), bf(row_b), bf(ones), bf(np.eye(256)), bf(slab))
+def along(axis, size):
+    return lax.broadcasted_iota(jnp.int32, (size, 1) if axis == 0 else (1, size), axis)
+
+
+def token_of(p):
+    return ((((p >> 4) & 1) * 2 + (p >> 6)) << 5) + (p & 15) * 2 + ((p >> 5) & 1)
+
+
+def place_of(t):
+    r, c = t >> 5, t & 31
+    return ((r & 1) * 2 + (c & 1)) * 32 + (r >> 1) * 16 + (c >> 1)
+
+
+def third(k):
+    return (k * 11) >> 5
+
+
+def slot_token(i):
+    s, k = i >> 4, i & 15
+    r = third(k) + jnp.where((s == 2) | (s == 3), 1, 0)
+    c = k - 3 * third(k) + jnp.where((s & 1) == 0, 29, 0)
+    return jnp.where(k < jnp.where(s < 2, 12, 9), r * 32 + c, -1)
+
+
+def sent_token(k):
+    return jnp.where(k < 96, k + 32, jnp.where(k < 192, k - 96, slot_token(k - 192)))
+
+
+def row_a_of(n):
+    return ((((n >> 2) & 7) * 2 + ((n >> 1) & 1)) * 4 + ((n >> 5) & 3)) * 4 + (n >> 7) * 2 + (n & 1)
+
+
+def row_b_of(n):
+    return ((n >> 4) & 1) * 128 + ((n >> 3) & 1) * 64 + ((n >> 5) & 3) * 16 + (n >> 7) * 8 + (n & 7)
+
+
+def slab_of(n):
+    return ((n >> 2) & 3) * 32 + (n >> 4) * 4 + (n & 3)
+
+
+def one_hot(rows, cols):
+    return jnp.where(rows == cols, 1.0, 0.0).astype(BF16)
+
+
+def allowed_keys(row, col):
+    n, p = along(0, NK), along(1, 128)
+    own = token_of(n)
+    i = n - 320
+    s, k = i >> 4, i & 15
+    slot_r = third(k) + jnp.where(s < 2, 0, jnp.where(s < 4, -3, 4))
+    slot_c = k - 3 * third(k) + jnp.where((s & 1) == 0, -3, 32)
+    slot_r = jnp.where(k < jnp.where(s < 2, 12, 9), slot_r, 1000)
+    side = jnp.where(n < 224, n - 128, n - 224)
+    kr = jnp.where(n < 128, own >> 5, jnp.where(n < 320, (side >> 5) + jnp.where(n < 224, -3, 4), slot_r))
+    kc = jnp.where(n < 128, own & 31, jnp.where(n < 320, side & 31, slot_c))
+    inside = (kr + 4 * row >= 0) & (kr + 4 * row < 4 * ROWS) & (kc + 32 * col >= 0) & (kc + 32 * col < 32 * COLS)
+    kr = jnp.where(inside, kr, 1000)
+    query = token_of(p)
+    return jnp.where((jnp.abs(kr - (query >> 5)) <= 3) & (jnp.abs(kc - (query & 31)) <= 3), 1.0, 0.0)
 
 
 def nt(a, b):
@@ -167,10 +174,22 @@
     return inverse, (x * inverse * gain).astype(BF16)
 
 
-def body(tokens, gain, w_qkv, head_scale, w_out, w_merge, d_merged, d_skip,
-         order, unorder, pick, back, near_mask, row_a, row_b, ones_t, eye, slab,
+def body(*refs):
+    sources, targets, held, ready, (load_sem, save_sem), work = (
+        refs[:8], refs[8:16], refs[16:24], refs[24:32], refs[32:34], refs[34:])
+    loads = [pltpu.make_async_copy(s, t, load_sem.at[i]) for i, (s, t) in enumerate(zip(sources, held))]
+    saves = [pltpu.make_async_copy(s, t, save_sem.at[i]) for i, (s, t) in enumerate(zip(ready, targets))]
+    for i in FIRST:
+        loads[i].start()
+    compute(loads, saves, *held, *ready, *work)
+
+
+FIRST = (0, 2, 1, 3, 6, 7, 5, 4)
+
+
+def compute(loads, saves, tokens, gain, w_qkv, head_scale, w_out, w_merge, d_merged, d_skip,
          o_skip, o_merged, o_tokens, o_qkv, o_out, o_merge, o_gain, o_scale,
-         xk, strips, kv, kvt, st, pt, ptb, dst, q4, da4, keep, hs, hr, rhs, allowed,
+         xk, strips, row_a, row_b, ones_t, kv, kvt, st, pt, ptb, dst, q4, da4, keep, hs, hr, rhs, allowed,
          ga, ra1, sa2, ra2, sa3, ra3, sa4, ra4,
          gb, rb1, sb2, rb2, sb3, rb3, sb4, rb4,
          g1, g2, g3, g4, tsem_a, tsem_b, tsem_g, tsem_h):
@@ -199,7 +218,21 @@
             for i, (dev, s, t) in enumerate(zip(devices, sources, targets))
         ])
 
-    strips[...] = moved(pick[...], tokens[...])
+    def loaded(*names):
+        for i in names:
+            loads[i].wait()
+
+    token_row = along(1, 128)
+    pick = one_hot(slot_token(along(0, 96)), token_row)
+    loaded(0)
+    strips[...] = moved(pick, tokens[...])
+    order = one_hot(token_of(along(0, 128)), token_row)
+    feature = along(1, 256)
+    row_a[...] = one_hot(row_a_of(along(0, 256)), feature)
+    row_b[...] = one_hot(row_b_of(along(0, 256)), feature)
+    ones_t[...] = one_hot(along(0, 256) >> 6, feature >> 6)
+    allowed[...] = allowed_keys(row, col)
+    rhs[...] = jnp.zeros_like(rhs)
     pl.semaphore_wait(bar, 8 + 1 + 3 + 7 + 7)
     spans = [pl.ds(0, 96), pl.ds(96, 96)] + [pl.ds(192 + 16 * s, 16) for s in range(6)]
     ch = halo(
@@ -208,13 +241,14 @@
         [xk.at[s] for s in spans],
     )
 
+    loaded(1, 2, 3)
     ones = ones_t[...]
     gains = gain[...]
     lane = lax.broadcasted_iota(jnp.int32, (1, 256), 1) // 64
     scales = jnp.zeros((1, 256), F32)
     for h in range(4):
-        scales = jnp.where(lane == h, head_scale[h], scales)
-    xp = moved(order[...], tokens[...])
+        scales = jnp.where(lane == h, head_scale[:, h : h + 1], scales)
+    xp = moved(order, tokens[...])
     x = xp.astype(F32)
     inverse, normed = norm_rows(x, gains)
     qkv = nn(normed, w_qkv[...])
@@ -230,22 +264,15 @@
     for h in range(4):
         q4[128 * h : 128 * h + 128] = jnp.where(lane == h, q_hat, zero)
 
+    loaded(4, 5, 6, 7)
     d_group = nt(d_merged[...], w_merge[...])
-    d_y = moved(order[...], d_skip[...]).astype(F32) + jnp.concatenate(
+    d_y = moved(order, d_skip[...]).astype(F32) + jnp.concatenate(
         [d_group[:, 256 * g : 256 * g + 256] for g in range(4)], axis=0)
     dy_b = d_y.astype(BF16)
     keep[4] = d_y
     d_attn = nt(dy_b, w_out[...]).astype(BF16)
     for h in range(4):
         da4[128 * h : 128 * h + 128] = jnp.where(lane == h, d_attn, zero)
-
-    yes = lambda c: jnp.where(c, 1.0, 0.0).astype(F32)
-    v_up, v_down, v_left, v_right = yes(row > 0), yes(row < ROWS - 1), yes(col > 0), yes(col < COLS - 1)
-    factors = [(128, 96, v_up), (224, 96, v_down), (320, 16, v_left), (336, 16, v_right),
-               (352, 16, v_up * v_left), (368, 16, v_up * v_right), (384, 16, v_down * v_left), (400, 16, v_down * v_right)]
-    allowed[:OWN] = near_mask[:OWN]
-    for at, size, f in factors:
-        allowed[at : at + size] = near_mask[at : at + size] * f
 
     wait_copies(ch)
     _, normed_h = norm_rows(xk[...].astype(F32), gains)
@@ -261,8 +288,9 @@
         p = e * (1.0 / jnp.sum(e, axis=0, keepdims=True))
         pt[:, span] = p
         ptb[:, span] = p.astype(BF16)
-    kvt[:256] = nt(eye[...], kv[:, :256]).astype(BF16)
-    kvt[256:] = nt(eye[...], kv[:, 256:]).astype(BF16)
+    eye = one_hot(along(0, 256), feature)
+    kvt[:256] = nt(eye, kv[:, :256]).astype(BF16)
+    kvt[256:] = nt(eye, kv[:, 256:]).astype(BF16)
 
     def diagonal(full):
         return jnp.concatenate([full[64 * h : 64 * h + 64, 128 * h : 128 * h + 128] for h in range(4)], axis=0).T
@@ -276,9 +304,11 @@
             gb[c, g] = part[:, 128 * c : 128 * c + 128].astype(BF16)
     mine = lambda size, index: pl.ds(pl.multiple_of(index * size, size), size)
     cb = exchange(near["core"][1], lambda t: gb.at[:, :, mine(128, t), :], rb1, *sems(tsem_b, 0))
-    o_skip[...] = moved(unorder[...], skip)
+    o_skip[...] = moved(one_hot(place_of(along(0, 128)), token_row), skip)
     group = jnp.concatenate([skip[32 * g : 32 * g + 32] for g in range(4)], axis=1)
     o_merged[...] = nn(group, w_merge[...]).astype(BF16)
+    saves[0].start()
+    saves[1].start()
 
     st[...] = nt(kv[:, 256:], da4[...])
     for h in range(4):
@@ -301,13 +331,12 @@
     g_u = d_qhat * scales
     d_q = (keep[0] * (g_u - u * head_sums(u * g_u, ones))).astype(BF16)
     lhs = jnp.concatenate([nt(row_a[...], normed), nt(row_a[...], attn)], axis=1).astype(BF16)
-    rhs[...] = jnp.zeros_like(rhs)
     dy_b = keep[4].astype(BF16)
     for c in range(4):
         rhs[128:, 256 * c + 192 : 256 * c + 256] = dy_b[:, 64 * c : 64 * c + 64]
 
     wait_copies(ch)
-    added = nn(back[...], hr[...])
+    added = nn(one_hot(token_of(along(0, 128)), sent_token(along(1, HALO))), hr[...])
     d_k = d_k + added[:, :256]
     d_v = d_v + added[:, 256:]
     ku = keep[3]
@@ -329,7 +358,8 @@
 
     scaled = gains * d_normed
     g_x = inverse * scaled - x * (inverse * inverse * inverse) * jnp.mean(x * scaled, axis=-1, keepdims=True)
-    o_tokens[...] = moved(unorder[...], (keep[4] + g_x).astype(BF16))
+    o_tokens[...] = moved(one_hot(place_of(along(0, 128)), token_row), (keep[4] + g_x).astype(BF16))
+    saves[2].start()
 
     wait_copies(ca)
     sa2[...] = (ga[:, mine(128, core), :].astype(F32) + ra1[0].astype(F32)).astype(BF16)
@@ -348,7 +378,7 @@
     total = sa2[:, mine(32, x_at), :].astype(F32)
     for p in range(3):
         total = total + ra2[p].astype(F32)
-    sa3[...] = moved(slab[...], total.astype(BF16).reshape(128, 256)).reshape(8, 16, 256)
+    sa3[...] = moved(one_hot(slab_of(along(0, 128)), token_row), total.astype(BF16).reshape(128, 256)).reshape(8, 16, 256)
     ca = exchange(near["y"][1], lambda t: sa3.at[t], ra3, *sems(tsem_a, 2))
     wait_copies(cg)
     g3[y_at] = (g2[0] + g2[1]) + (g2[2] + g2[3])
@@ -374,6 +404,7 @@
     for p in range(7):
         total = total + rb4[p]
     o_merge[...] = total
+    saves[5].start()
 
     wait_copies(ca)
     total = sa4[z_at // 4]
@@ -385,6 +416,8 @@
         piece = piece + jnp.where(part == i, total[2 * i : 2 * i + 2], 0.0)
     o_qkv[...] = piece[:, :192]
     o_out[...] = piece[:, 192:]
+    saves[3].start()
+    saves[4].start()
     wait_copies(cg)
     total = ((g4[0] + g4[1]) + (g4[2] + g4[3])) + ((g4[4] + g4[5]) + (g4[6] + g4[7]))
     o_gain[...] = total[0:2]
@@ -394,25 +427,39 @@
         r = total[2 + h // 2 : 3 + h // 2]
         s = jnp.sum(jnp.where(halves // 64 == h % 2, r, 0.0), axis=1, keepdims=True)
         out = jnp.where(halves == h, s, out)
-    o_scale[...] = out
+    o_scale[...] = out[:, :4]
+    saves[6].start()
+    saves[7].start()
+    wait_copies(saves)
+
+
+def hand_over(*refs):
+    sources, targets, sem = refs[:8], refs[8:16], refs[16]
+    wait_copies(start_copies(
+        [pltpu.make_async_copy(s, t, sem.at[i]) for i, (s, t) in enumerate(zip(sources, targets))]))
 
 
 def on_device(tokens, gain, w_qkv, head_scale, w_out, w_merge, d_merged, d_skip):
     V = pltpu.VMEM
     S = jax.ShapeDtypeStruct
-    vmem = pl.BlockSpec(memory_space=V)
-    smem = pl.BlockSpec(memory_space=pltpu.SMEM)
     DMA = pltpu.SemaphoreType.DMA
+    operands = (
+        tokens.reshape(128, 256), gain.reshape(1, 256), w_qkv, head_scale.reshape(1, 4), w_out, w_merge,
+        d_merged.reshape(32, 512), d_skip.reshape(128, 256),
+    )
+    results = (
+        S((128, 256), BF16), S((32, 512), BF16), S((128, 256), BF16),
+        S((2, 192), F32), S((2, 64), F32), S((8, 128), F32), S((2, 128), F32), S((1, 4), F32),
+    )
+    far = pl.BlockSpec(memory_space=pltpu.MemorySpace.HBM)
     out = pl.pallas_call(
         body,
-        out_shape=(
-            S((128, 256), BF16), S((32, 512), BF16), S((128, 256), BF16),
-            S((2, 192), F32), S((2, 64), F32), S((8, 128), F32), S((2, 128), F32), S((1, 128), F32),
-        ),
-        in_specs=[vmem] * 3 + [smem] + [vmem] * 14,
-        out_specs=(vmem,) * 8,
-        scratch_shapes=[
-            V((HALO, 256), BF16), V((96, 256), BF16), V((NK, 512), BF16), V((512, NK), BF16),
+        out_shape=results,
+        in_specs=[far] * 8,
+        out_specs=(far,) * 8,
+        scratch_shapes=[V(a.shape, a.dtype) for a in operands + results] + [
+            DMA((8,)), DMA((8,)),
+            V((HALO, 256), BF16), V((96, 256), BF16), V((256, 256), BF16), V((256, 256), BF16), V((256, 256), BF16), V((NK, 512), BF16), V((512, NK), BF16),
             V((NK, 512), F32), V((NK, 512), F32), V((NK, 512), BF16), V((NK, 512), BF16),
             V((512, 256), BF16), V((512, 256), BF16), V((5, 128, 256), F32),
             V((HALO, 512), BF16), V((HALO, 512), BF16), V((256, 1024), BF16), V((NK, 128), F32),
@@ -427,13 +474,18 @@
             V((2, 8, 128), F32), V((4, 8, 128), F32), V((8, 8, 128), F32), V((8, 8, 128), F32),
             DMA((2, 28)), DMA((2, 28)), DMA((2, 28)), DMA((2, 16)),
         ],
-        compiler_params=pltpu.CompilerParams(collective_id=0, has_side_effects=True, vmem_limit_bytes=48 * 2**20),
-    )(
-        tokens.reshape(128, 256), gain.reshape(1, 256), w_qkv, head_scale, w_out, w_merge,
-        d_merged.reshape(32, 512), d_skip.reshape(128, 256), *tables(),
-    )
+        compiler_params=pltpu.CompilerParams(collective_id=0, has_side_effects=True, vmem_limit_bytes=VMEM_LIMIT),
+    )(*operands)
+    out = pl.pallas_call(
+        hand_over,
+        out_shape=results,
+        in_specs=[far] * 8,
+        out_specs=(far,) * 8,
+        scratch_shapes=[DMA((8,))],
+        compiler_params=pltpu.CompilerParams(vmem_limit_bytes=VMEM_LIMIT),
+    )(*out)
     skip, merged, grad, qkv, o, m, g, s = out
-    return (skip.reshape(4, 32, 256), merged.reshape(2, 16, 512), grad.reshape(4, 32, 256), qkv, o, m, g.reshape(256), s[0, :4])
+    return (skip.reshape(4, 32, 256), merged.reshape(2, 16, 512), grad.reshape(4, 32, 256), qkv, o, m, g.reshape(256), s.reshape(4))
 
 
 def solution(mesh):

time: 70.5 us -> 57 us (0.81)
  local copies, waits for them, and re-layouts: 19.4 us -> 0 us
  Pallas kernels: 49.7 us -> 56.2 us
    unnamed x43 -> x0, local copies, waits for them, and re-layouts: 18.8 us -> none
    pallas_call x1 -> x2, Pallas kernels: 49.7 us -> 56.2 us  [the longest x1 49.8 us: on_device(): pl.pallas_call(body, out_shape=results, in_specs=[far] * 8, out_specs=(fa...]
where the time goes in v3:
time: 57 us; the launch traced here: 56.9 us
  Pallas kernels  56.2 us (99%)
  between operations  0.64 us (1%)
    pallas_call x1, Pallas kernels, on_device(): pl.pallas_call(body, out_shape=results, in_specs=[far] * 8, out_specs=(fa...  49.8 us
    pallas_call x1, Pallas kernels, on_device(): pl.pallas_call(hand_over, out_shape=results, in_specs=[far] * 8, out_spec...  6.4 us

profile of v3, /device:TPU:6, one launch (start us, length us, event | category | flops | bytes accessed | tf_op | source)
XLA Modules:
  0.0 56.9 jit_solution(10679381234322479587)
XLA Ops:
  0.6 49.8 %shard_map.143 = (bf16[128,256]{1,0:T(8,128)(2,1)}, bf16[32,512]{1,0:T(8,128)(2,1)}, bf16[128,256]{1,0:T(8,128)(2,1)}, f32[2,192]{1,0:T(2,128)}, f32[2,64]{1,0:T...) custom-call(bf16[128,256]{1,0:T(8,128)(2,1)} %bitcast.10, f32[1,256]{1,0:T(1,128)} %bitcast.13, ...), custom_call_target="tpu_custom_call" | custom-call | tf_op jit(solution)/shard_map/pallas_call | solution.py:455
  50.5 6.4 %shard_map.144 = (bf16[128,256]{1,0:T(8,128)(2,1)}, bf16[32,512]{1,0:T(8,128)(2,1)}, bf16[128,256]{1,0:T(8,128)(2,1)}, f32[2,192]{1,0:T(2,128)}, f32[2,64]{1,0:T...) custom-call(bf16[128,256]{1,0:T(8,128)(2,1)} %get-tuple-element.24.refs_0_, ...), custom_call_target="tpu_custom_call" | custom-call | tf_op jit(solution)/shard_map/pallas_call | solution.py:479

commit v4 on v3

--- a/solution.py
+++ b/solution.py
@@ -86,10 +86,6 @@
     )
 
 
-def rows_at(ref, index, size):
-    return ref.at[:, pl.ds(pl.multiple_of(index * size, size), size), :]
-
-
 def along(axis, size):
     return lax.broadcasted_iota(jnp.int32, (size, 1) if axis == 0 else (1, size), axis)
 
@@ -123,7 +119,7 @@
 
 
 def row_b_of(n):
-    return ((n >> 4) & 1) * 128 + ((n >> 3) & 1) * 64 + ((n >> 5) & 3) * 16 + (n >> 7) * 8 + (n & 7)
+    return ((n >> 3) & 1) * 64 + ((n >> 4) & 3) * 16 + (n >> 6) * 8 + (n & 7)
 
 
 def slab_of(n):
@@ -189,10 +185,10 @@
 
 def compute(loads, saves, tokens, gain, w_qkv, head_scale, w_out, w_merge, d_merged, d_skip,
          o_skip, o_merged, o_tokens, o_qkv, o_out, o_merge, o_gain, o_scale,
-         xk, strips, row_a, row_b, ones_t, kv, kvt, st, pt, ptb, dst, q4, da4, keep, hs, hr, rhs, allowed,
+         xk, strips, row_a, row_b, ones_t, kv, kvt, st, pt, ptb, dst, q4, da4, keep, keys, xhat, nt_all, hs, hr, allowed,
          ga, ra1, sa2, ra2, sa3, ra3, sa4, ra4,
-         gb, rb1, sb2, rb2, sb3, rb3, sb4, rb4,
-         g1, g2, g3, g4, tsem_a, tsem_b, tsem_g, tsem_h):
+         skips, gx, dmx, gb, rb1, sb2, rb2, sb4, rb4,
+         g1, g2, g3, g4, tsem_a, tsem_b, tsem_d, tsem_g, tsem_h):
     near = peers()
     core, x_at, y_at, z_at = (near[a][0] for a in ("core", "x", "y", "z"))
     row, col = lax.axis_index("row"), lax.axis_index("col")
@@ -229,10 +225,9 @@
     order = one_hot(token_of(along(0, 128)), token_row)
     feature = along(1, 256)
     row_a[...] = one_hot(row_a_of(along(0, 256)), feature)
-    row_b[...] = one_hot(row_b_of(along(0, 256)), feature)
+    row_b[...] = one_hot(row_b_of(along(0, 128)), token_row)
     ones_t[...] = one_hot(along(0, 256) >> 6, feature >> 6)
     allowed[...] = allowed_keys(row, col)
-    rhs[...] = jnp.zeros_like(rhs)
     pl.semaphore_wait(bar, 8 + 1 + 3 + 7 + 7)
     spans = [pl.ds(0, 96), pl.ds(96, 96)] + [pl.ds(192 + 16 * s, 16) for s in range(6)]
     ch = halo(
@@ -240,6 +235,10 @@
         [tokens.at[pl.ds(32, 96)], tokens.at[pl.ds(0, 96)]] + [strips.at[pl.ds(16 * s, 16)] for s in range(6)],
         [xk.at[s] for s in spans],
     )
+
+    loaded(6)
+    dmx[7] = d_merged[...]
+    cd = exchange(near["y"][1], lambda t: d_merged, dmx, tsem_d.at[0], tsem_d.at[1])
 
     loaded(1, 2, 3)
     ones = ones_t[...]
@@ -251,34 +250,41 @@
     xp = moved(order, tokens[...])
     x = xp.astype(F32)
     inverse, normed = norm_rows(x, gains)
+    xhat[:OWN] = x * inverse
+    nt_all[:, :OWN] = nt(row_a[...], normed).astype(BF16)
     qkv = nn(normed, w_qkv[...])
     q, k = qkv[:, :256], qkv[:, 256:512]
     q_norm = lax.rsqrt(head_sums(q * q, ones) + EPS)
     k_norm = lax.rsqrt(head_sums(k * k, ones) + EPS)
     q_unit, k_unit = q * q_norm, k * k_norm
     q_hat = (q_unit * scales).astype(BF16)
-    keep[0], keep[1], keep[2], keep[3] = q_norm, k_norm, q_unit, k_unit
+    keep[0], keep[1] = q_norm, q_unit
+    keys[0, :OWN], keys[1, :OWN] = k_norm, k_unit
     kv[:OWN, :256] = k_unit.astype(BF16)
     kv[:OWN, 256:] = qkv[:, 512:].astype(BF16)
     zero = jnp.zeros((), BF16)
     for h in range(4):
         q4[128 * h : 128 * h + 128] = jnp.where(lane == h, q_hat, zero)
 
-    loaded(4, 5, 6, 7)
+    loaded(4, 5, 7)
     d_group = nt(d_merged[...], w_merge[...])
     d_y = moved(order, d_skip[...]).astype(F32) + jnp.concatenate(
         [d_group[:, 256 * g : 256 * g + 256] for g in range(4)], axis=0)
     dy_b = d_y.astype(BF16)
-    keep[4] = d_y
+    keep[2] = d_y
     d_attn = nt(dy_b, w_out[...]).astype(BF16)
     for h in range(4):
         da4[128 * h : 128 * h + 128] = jnp.where(lane == h, d_attn, zero)
 
     wait_copies(ch)
-    _, normed_h = norm_rows(xk[...].astype(F32), gains)
+    xh = xk[...].astype(F32)
+    inverse_h, normed_h = norm_rows(xh, gains)
     kv_h = nn(normed_h, w_qkv[:, 256:])
     k_h = kv_h[:, :256]
-    kv[OWN:, :256] = (k_h * lax.rsqrt(head_sums(k_h * k_h, ones) + EPS)).astype(BF16)
+    k_norm_h = lax.rsqrt(head_sums(k_h * k_h, ones) + EPS)
+    k_unit_h = k_h * k_norm_h
+    keys[0, OWN:], keys[1, OWN:] = k_norm_h, k_unit_h
+    kv[OWN:, :256] = k_unit_h.astype(BF16)
     kv[OWN:, 256:] = kv_h[:, 256:].astype(BF16)
 
     st[...] = nt(kv[:, :256], q4[...])
@@ -288,107 +294,107 @@
         p = e * (1.0 / jnp.sum(e, axis=0, keepdims=True))
         pt[:, span] = p
         ptb[:, span] = p.astype(BF16)
-    eye = one_hot(along(0, 256), feature)
-    kvt[:256] = nt(eye, kv[:, :256]).astype(BF16)
-    kvt[256:] = nt(eye, kv[:, 256:]).astype(BF16)
-
-    def diagonal(full):
-        return jnp.concatenate([full[64 * h : 64 * h + 64, 128 * h : 128 * h + 128] for h in range(4)], axis=0).T
-
-    attn = diagonal(nn(kvt[256:], ptb[...])).astype(BF16)
-    skip = (x + nn(attn, w_out[...])).astype(BF16)
-    dm = d_merged[...]
-    for g in range(4):
-        part = nn(nt(row_b[...], skip[32 * g : 32 * g + 32]).astype(BF16), dm)
-        for c in range(4):
-            gb[c, g] = part[:, 128 * c : 128 * c + 128].astype(BF16)
-    mine = lambda size, index: pl.ds(pl.multiple_of(index * size, size), size)
-    cb = exchange(near["core"][1], lambda t: gb.at[:, :, mine(128, t), :], rb1, *sems(tsem_b, 0))
-    o_skip[...] = moved(one_hot(place_of(along(0, 128)), token_row), skip)
-    group = jnp.concatenate([skip[32 * g : 32 * g + 32] for g in range(4)], axis=1)
-    o_merged[...] = nn(group, w_merge[...]).astype(BF16)
-    saves[0].start()
-    saves[1].start()
 
     st[...] = nt(kv[:, 256:], da4[...])
     for h in range(4):
         span = slice(128 * h, 128 * h + 128)
         dw, p = st[:, span], pt[:, span]
         dst[:, span] = (p * (dw - jnp.sum(dw * p, axis=0, keepdims=True))).astype(BF16)
-    hs[:, :256] = nn(dst[OWN:], q4[...]).astype(BF16)
-    hs[:, 256:] = nn(ptb[OWN:], da4[...]).astype(BF16)
-    ch = halo(1, reverse, [hs.at[s] for s in spans], [hr.at[s] for s in spans])
-
-    wait_copies(cb)
-    sb2[...] = (gb[:, :, mine(128, core), :].astype(F32) + rb1[0].astype(F32)).astype(BF16)
-    cb = exchange(near["x"][1], lambda t: sb2.at[:, :, mine(32, t), :], rb2, *sems(tsem_b, 1))
-
-    d_k = nn(dst[:OWN], q4[...])
-    d_v = nn(ptb[:OWN], da4[...])
-    d_qhat = diagonal(nn(kvt[:256], dst[...]))
-    u = keep[2]
-    scale_row = jnp.sum(u * d_qhat, axis=0, keepdims=True)
+    d_k = nn(dst[...], q4[...])
+    ku = keys[1]
+    d_kraw = (keys[0] * (d_k - ku * head_sums(ku * d_k, ones))).astype(BF16)
+    d_v = nn(ptb[...], da4[...]).astype(BF16)
+    nt_all[:, OWN:] = nt(row_a[...], normed_h).astype(BF16)
+    normed_t = nt_all[...]
+    eye = one_hot(along(0, 256), feature)
+    kvt[:256] = nt(eye, kv[:, :256]).astype(BF16)
+    kvt[256:] = nt(eye, kv[:, 256:]).astype(BF16)
+
+    def diagonal(full):
+        return jnp.concatenate([full[64 * h : 64 * h + 64, 128 * h : 128 * h + 128] for h in range(4)], axis=0)
+
+    d_qhat = diagonal(nn(kvt[:256], dst[...])).T
+    u = keep[1]
     g_u = d_qhat * scales
     d_q = (keep[0] * (g_u - u * head_sums(u * g_u, ones))).astype(BF16)
-    lhs = jnp.concatenate([nt(row_a[...], normed), nt(row_a[...], attn)], axis=1).astype(BF16)
-    dy_b = keep[4].astype(BF16)
-    for c in range(4):
-        rhs[128:, 256 * c + 192 : 256 * c + 256] = dy_b[:, 64 * c : 64 * c + 64]
-
-    wait_copies(ch)
-    added = nn(one_hot(token_of(along(0, 128)), sent_token(along(1, HALO))), hr[...])
-    d_k = d_k + added[:, :256]
-    d_v = d_v + added[:, 256:]
-    ku = keep[3]
-    d_kraw = (keep[1] * (d_k - ku * head_sums(ku * d_k, ones))).astype(BF16)
-    d_qkv = jnp.concatenate([d_q, d_kraw, d_v.astype(BF16)], axis=1)
-    for c in range(4):
-        rhs[:128, 256 * c : 256 * c + 192] = d_qkv[:, 192 * c : 192 * c + 192]
-    for c in range(4):
-        ga[c] = nn(lhs, rhs[:, 256 * c : 256 * c + 256]).astype(BF16)
-    ca = exchange(near["core"][1], lambda t: rows_at(ga, t, 128), ra1, *sems(tsem_a, 0))
-
-    d_normed = nt(d_qkv, w_qkv[...])
-    x = xp.astype(F32)
-    gain_row = jnp.sum(x * inverse * d_normed, axis=0, keepdims=True)
+    attn_t = diagonal(nn(kvt[256:], ptb[...]))
+    ga[:, :256] = nn(normed_t[:, :OWN], d_q).astype(BF16)
+    ga[:, 256:512] = nn(normed_t, d_kraw).astype(BF16)
+    ga[:, 512:768] = nn(normed_t, d_v).astype(BF16)
+    ga[:, 768:] = nn(nn(row_a[...], attn_t.astype(BF16)).astype(BF16), keep[2].astype(BF16)).astype(BF16)
+    mine = lambda size, index: pl.ds(pl.multiple_of(index * size, size), size)
+    ca = exchange(near["core"][1], lambda t: ga.at[mine(128, t)], ra1, *sems(tsem_a, 0))
+
+    attn = attn_t.T.astype(BF16)
+    skip = (xp.astype(F32) + nn(attn, w_out[...])).astype(BF16)
+    skips[...] = skip
+    cb = exchange(
+        near["y"][1], lambda t: skips.at[mine(32, t // 2), mine(128, t % 2)], gx, tsem_b.at[0, :7], tsem_b.at[1, :7])
+
+    d_normed_h = nt(d_kraw[OWN:], w_qkv[:, 256:512]) + nt(d_v[OWN:], w_qkv[:, 512:])
+    hs[...] = d_normed_h.astype(BF16)
+    ch = halo(1, reverse, [hs.at[s] for s in spans], [hr.at[s] for s in spans])
+    wait_copies(ca)
+    sa2[...] = (ga[mine(128, core)].astype(F32) + ra1[0].astype(F32)).astype(BF16)
+    ca = exchange(near["x"][1], lambda t: sa2.at[mine(32, t)], ra2, *sems(tsem_a, 1))
+
+    d_normed = (nt(d_q, w_qkv[:, :256]) + nt(d_kraw[:OWN], w_qkv[:, 256:512])) + nt(d_v[:OWN], w_qkv[:, 512:])
+    gain_row = jnp.sum(xhat[:OWN] * d_normed, axis=0, keepdims=True) + jnp.sum(
+        xh * inverse_h * d_normed_h, axis=0, keepdims=True)
+    scale_row = jnp.sum(u * d_qhat, axis=0, keepdims=True)
     for i, r in enumerate((gain_row[:, :128], gain_row[:, 128:], scale_row[:, :128], scale_row[:, 128:])):
         g1[core, i : i + 1] = r
     g1[core, 4:8] = jnp.zeros((4, 128), F32)
     cg = spread(core, near["core"][1], g1, *sems(tsem_g, 0))
 
-    scaled = gains * d_normed
-    g_x = inverse * scaled - x * (inverse * inverse * inverse) * jnp.mean(x * scaled, axis=-1, keepdims=True)
-    o_tokens[...] = moved(one_hot(place_of(along(0, 128)), token_row), (keep[4] + g_x).astype(BF16))
-    saves[2].start()
-
-    wait_copies(ca)
-    sa2[...] = (ga[:, mine(128, core), :].astype(F32) + ra1[0].astype(F32)).astype(BF16)
-    ca = exchange(near["x"][1], lambda t: rows_at(sa2, t, 32), ra2, *sems(tsem_a, 1))
+    unorder = one_hot(place_of(along(0, 128)), token_row)
+    o_skip[...] = moved(unorder, skip)
+    group = jnp.concatenate([skip[32 * g : 32 * g + 32] for g in range(4)], axis=1)
+    o_merged[...] = nn(group, w_merge[...]).astype(BF16)
+    saves[0].start()
+    saves[1].start()
     wait_copies(cg)
     g2[x_at] = g1[0] + g1[1]
     cg = spread(x_at, near["x"][1], g2, *sems(tsem_g, 1))
+
+    gx[7] = skips[mine(32, y_at // 2), mine(128, y_at % 2)]
+    wait_copies(cd)
     wait_copies(cb)
-    total = sb2[:, :, mine(32, x_at), :].astype(F32)
-    for p in range(3):
-        total = total + rb2[p].astype(F32)
-    sb3[...] = total.astype(BF16)
-    cb = exchange(near["y"][1], lambda t: sb3.at[:, t // 2, mine(16, t % 2), :], rb3, *sems(tsem_b, 2))
+    factor = nt(row_b[...], gx[...].reshape(256, 128)).astype(BF16)
+    gb[...] = nn(factor, dmx[...].reshape(256, 512)).astype(BF16)
+    cb = exchange(near["core"][1], lambda t: gb.at[mine(64, t)], rb1, tsem_b.at[0, 7:8], tsem_b.at[1, 7:8])
 
     wait_copies(ca)
-    total = sa2[:, mine(32, x_at), :].astype(F32)
+    total = sa2[mine(32, x_at)].astype(F32)
     for p in range(3):
         total = total + ra2[p].astype(F32)
-    sa3[...] = moved(one_hot(slab_of(along(0, 128)), token_row), total.astype(BF16).reshape(128, 256)).reshape(8, 16, 256)
+    total = jnp.concatenate(
+        [jnp.concatenate([total[:, 192 * c : 192 * c + 192], total[:, 768 + 64 * c : 832 + 64 * c]], axis=1)
+         for c in range(4)], axis=0)
+    sa3[...] = moved(one_hot(slab_of(along(0, 128)), token_row), total.astype(BF16)).reshape(8, 16, 256)
     ca = exchange(near["y"][1], lambda t: sa3.at[t], ra3, *sems(tsem_a, 2))
     wait_copies(cg)
     g3[y_at] = (g2[0] + g2[1]) + (g2[2] + g2[3])
     cg = spread(y_at, near["y"][1], g3, *sems(tsem_g, 2))
     wait_copies(cb)
-    total = sb3[:, y_at // 2, mine(16, y_at % 2), :].astype(F32)
-    for p in range(7):
-        total = total + rb3[p].astype(F32)
+    sb2[...] = (gb[mine(64, core)].astype(F32) + rb1[0].astype(F32)).astype(BF16)
+    cb = exchange(near["x"][1], lambda t: sb2.at[mine(16, t)], rb2, tsem_b.at[0, 8:11], tsem_b.at[1, 8:11])
+
+    wait_copies(ch)
+    d_normed = d_normed + nn(one_hot(token_of(along(0, 128)), sent_token(along(1, HALO))), hr[...])
+    scaled = gains * d_normed
+    x = xp.astype(F32)
+    g_x = inverse * scaled - x * (inverse * inverse * inverse) * jnp.mean(x * scaled, axis=-1, keepdims=True)
+    o_tokens[...] = moved(unorder, (keep[2] + g_x).astype(BF16))
+    saves[2].start()
+
+    wait_copies(cb)
+    total = sb2[mine(16, x_at)].astype(F32)
+    for p in range(3):
+        total = total + rb2[p].astype(F32)
     sb4[...] = total
-    cb = exchange(near["z"][1], lambda t: sb4.at[t // 2, mine(8, t % 2), :], rb4, *sems(tsem_b, 3))
+    cb = exchange(
+        near["z"][1], lambda t: sb4.at[mine(8, t % 2), mine(128, t // 2)], rb4, tsem_b.at[0, 11:], tsem_b.at[1, 11:])
 
     wait_copies(ca)
     total = sa3[y_at].astype(F32)
@@ -399,13 +405,13 @@
     wait_copies(cg)
     g4[z_at] = ((g3[0] + g3[1]) + (g3[2] + g3[3])) + ((g3[4] + g3[5]) + (g3[6] + g3[7]))
     cg = spread(z_at, near["z"][1], g4, *sems(tsem_g, 3))
+
     wait_copies(cb)
-    total = sb4[z_at // 2, mine(8, z_at % 2), :]
+    total = sb4[mine(8, z_at % 2), mine(128, z_at // 2)]
     for p in range(7):
         total = total + rb4[p]
     o_merge[...] = total
     saves[5].start()
-
     wait_copies(ca)
     total = sa4[z_at // 4]
     for p in range(7):
@@ -425,8 +431,7 @@
     out = jnp.zeros((1, 128), F32)
     for h in range(4):
         r = total[2 + h // 2 : 3 + h // 2]
-        s = jnp.sum(jnp.where(halves // 64 == h % 2, r, 0.0), axis=1, keepdims=True)
-        out = jnp.where(halves == h, s, out)
+        out = jnp.where(halves == h, jnp.sum(jnp.where(halves // 64 == h % 2, r, 0.0), axis=1, keepdims=True), out)
     o_scale[...] = out[:, :4]
     saves[6].start()
     saves[7].start()
@@ -434,9 +439,13 @@
 
 
 def hand_over(*refs):
-    sources, targets, sem = refs[:8], refs[8:16], refs[16]
-    wait_copies(start_copies(
-        [pltpu.make_async_copy(s, t, sem.at[i]) for i, (s, t) in enumerate(zip(sources, targets))]))
+    sources, targets, held, sem = refs[:8], refs[8:16], refs[16:24], refs[24]
+    loads = start_copies([pltpu.make_async_copy(s, h, sem.at[0, i]) for i, (s, h) in enumerate(zip(sources, held))])
+    saves = [pltpu.make_async_copy(h, t, sem.at[1, i]) for i, (h, t) in enumerate(zip(held, targets))]
+    for load, save in zip(loads, saves):
+        load.wait()
+        save.start()
+    wait_copies(saves)
 
 
 def on_device(tokens, gain, w_qkv, head_scale, w_out, w_merge, d_merged, d_skip):
@@ -459,20 +468,21 @@
         out_specs=(far,) * 8,
         scratch_shapes=[V(a.shape, a.dtype) for a in operands + results] + [
             DMA((8,)), DMA((8,)),
-            V((HALO, 256), BF16), V((96, 256), BF16), V((256, 256), BF16), V((256, 256), BF16), V((256, 256), BF16), V((NK, 512), BF16), V((512, NK), BF16),
+            V((HALO, 256), BF16), V((96, 256), BF16), V((256, 256), BF16), V((128, 128), BF16), V((256, 256), BF16),
+            V((NK, 512), BF16), V((512, NK), BF16),
             V((NK, 512), F32), V((NK, 512), F32), V((NK, 512), BF16), V((NK, 512), BF16),
-            V((512, 256), BF16), V((512, 256), BF16), V((5, 128, 256), F32),
-            V((HALO, 512), BF16), V((HALO, 512), BF16), V((256, 1024), BF16), V((NK, 128), F32),
-            V((4, 256, 256), BF16), V((1, 4, 128, 256), BF16),
-            V((4, 128, 256), BF16), V((3, 4, 32, 256), BF16),
+            V((512, 256), BF16), V((512, 256), BF16), V((3, 128, 256), F32), V((2, NK, 256), F32), V((OWN, 256), F32),
+            V((256, NK), BF16), V((HALO, 256), BF16), V((HALO, 256), BF16), V((NK, 128), F32),
+            V((256, 1024), BF16), V((1, 128, 1024), BF16),
+            V((128, 1024), BF16), V((3, 32, 1024), BF16),
             V((8, 16, 256), BF16), V((7, 16, 256), BF16),
             V((2, 8, 256), F32), V((7, 8, 256), F32),
-            V((4, 4, 256, 128), BF16), V((1, 4, 4, 128, 128), BF16),
-            V((4, 4, 128, 128), BF16), V((3, 4, 4, 32, 128), BF16),
-            V((4, 4, 32, 128), BF16), V((7, 4, 16, 128), BF16),
-            V((4, 16, 128), F32), V((7, 8, 128), F32),
+            V((128, 256), BF16), V((8, 32, 128), BF16), V((8, 32, 512), BF16),
+            V((128, 512), BF16), V((1, 64, 512), BF16),
+            V((64, 512), BF16), V((3, 16, 512), BF16),
+            V((16, 512), F32), V((7, 8, 128), F32),
             V((2, 8, 128), F32), V((4, 8, 128), F32), V((8, 8, 128), F32), V((8, 8, 128), F32),
-            DMA((2, 28)), DMA((2, 28)), DMA((2, 28)), DMA((2, 16)),
+            DMA((2, 28)), DMA((2, 18)), DMA((2, 7)), DMA((2, 28)), DMA((2, 16)),
         ],
         compiler_params=pltpu.CompilerParams(collective_id=0, has_side_effects=True, vmem_limit_bytes=VMEM_LIMIT),
     )(*operands)
@@ -481,7 +491,7 @@
         out_shape=results,
         in_specs=[far] * 8,
         out_specs=(far,) * 8,
-        scratch_shapes=[DMA((8,))],
+        scratch_shapes=[V(a.shape, a.dtype) for a in results] + [DMA((2, 8))],
         compiler_params=pltpu.CompilerParams(vmem_limit_bytes=VMEM_LIMIT),
     )(*out)
     skip, merged, grad, qkv, o, m, g, s = out

time: 57 us -> 45.8 us (0.80); the launches traced: 56.9 us -> 45 us
  Pallas kernels: 56.2 us -> 44.3 us
    pallas_call x1, Pallas kernels: 49.8 us -> 42.6 us  [on_device(): pl.pallas_call(body, out_shape=results, in_specs=[far] * 8, out_specs=(fa...]
    pallas_call x1, Pallas kernels: 6.4 us -> 1.67 us  [on_device(): pl.pallas_call(hand_over, out_shape=results, in_specs=[far] * 8, out_spec...]
where the time goes in v4:
time: 45.8 us; the launch traced here: 45 us
  Pallas kernels  44.3 us (97%)
  between operations  0.64 us (1%)
    pallas_call x1, Pallas kernels, on_device(): pl.pallas_call(body, out_shape=results, in_specs=[far] * 8, out_specs=(fa...  42.6 us
    pallas_call x1, Pallas kernels, on_device(): pl.pallas_call(hand_over, out_shape=results, in_specs=[far] * 8, out_spec...  1.67 us

profile of v4, /device:TPU:6, one launch (start us, length us, event | category | flops | bytes accessed | tf_op | source)
XLA Modules:
  0.0 45.0 jit_solution(8449079061551321457)
XLA Ops:
  0.6 42.6 %shard_map.143 = (bf16[128,256]{1,0:T(8,128)(2,1)}, bf16[32,512]{1,0:T(8,128)(2,1)}, bf16[128,256]{1,0:T(8,128)(2,1)}, f32[2,192]{1,0:T(2,128)}, f32[2,64]{1,0:T...) custom-call(bf16[128,256]{1,0:T(8,128)(2,1)} %bitcast.10, f32[1,256]{1,0:T(1,128)} %bitcast.13, ...), custom_call_target="tpu_custom_call" | custom-call | tf_op jit(solution)/shard_map/pallas_call | solution.py:464
  43.3 1.7 %shard_map.144 = (bf16[128,256]{1,0:T(8,128)(2,1)}, bf16[32,512]{1,0:T(8,128)(2,1)}, bf16[128,256]{1,0:T(8,128)(2,1)}, f32[2,192]{1,0:T(2,128)}, f32[2,64]{1,0:T...) custom-call(bf16[128,256]{1,0:T(8,128)(2,1)} %get-tuple-element.24.refs_0_, ...), custom_call_target="tpu_custom_call" | custom-call | tf_op jit(solution)/shard_map/pallas_call | solution.py:489

commit v5 on v4

--- a/solution.py
+++ b/solution.py
@@ -17,11 +17,11 @@
 
 def place():
     row, col = lax.axis_index("row"), lax.axis_index("col")
-    return row // 16, (row // 8) % 2, (row // 2) % 4, row % 2, col
+    return row >> 4, (row >> 3) & 1, (row >> 1) & 3, row & 1, col
 
 
 def device(y, zl, x, core, col):
-    return (((y * 2 + zl) * 4 + x) * 2 + core, col)
+    return ((y << 4) | (zl << 3) | (x << 1) | core, col)
 
 
 def peers():
@@ -30,16 +30,16 @@
     out = {"core": (core, [(1 - core, device(y, zl, x, 1 - core, col))])}
     out["x"] = (x, [])
     for p in range(1, NX):
-        t = (x + p) % NX
+        t = (x + p) & (NX - 1)
         out["x"][1].append((t, device(y, zl, t, core, col)))
     out["y"] = (y, [])
     for p in range(1, NY):
-        t = (y + p) % NY
+        t = (y + p) & (NY - 1)
         out["y"][1].append((t, device(t, zl, x, core, col)))
     out["z"] = (z, [])
     for p in range(1, NZ):
-        t = (z + p) % NZ
-        out["z"][1].append((t, device(y, t % 2, x, core, t // 2)))
+        t = (z + p) & (NZ - 1)
+        out["z"][1].append((t, device(y, t & 1, x, core, t >> 1)))
     return out
 
 
@@ -52,6 +52,18 @@
 def wait_copies(copies):
     for c in copies:
         c.wait()
+
+
+def arrived(copies, sent):
+    for c in copies:
+        c.wait_recv()
+    sent.extend(copies)
+
+
+def drain(sent):
+    for c in sent:
+        c.wait_send()
+    sent.clear()
 
 
 def exchange(peer_list, source, slots, send, recv):
@@ -175,8 +187,6 @@
         refs[:8], refs[8:16], refs[16:24], refs[24:32], refs[32:34], refs[34:])
     loads = [pltpu.make_async_copy(s, t, load_sem.at[i]) for i, (s, t) in enumerate(zip(sources, held))]
     saves = [pltpu.make_async_copy(s, t, save_sem.at[i]) for i, (s, t) in enumerate(zip(ready, targets))]
-    for i in FIRST:
-        loads[i].start()
     compute(loads, saves, *held, *ready, *work)
 
 
@@ -190,15 +200,18 @@
          skips, gx, dmx, gb, rb1, sb2, rb2, sb4, rb4,
          g1, g2, g3, g4, tsem_a, tsem_b, tsem_d, tsem_g, tsem_h):
     near = peers()
+    sent = []
     core, x_at, y_at, z_at = (near[a][0] for a in ("core", "x", "y", "z"))
     row, col = lax.axis_index("row"), lax.axis_index("col")
-    up, down = (row + ROWS - 1) % ROWS, (row + 1) % ROWS
-    left, right = (col + COLS - 1) % COLS, (col + 1) % COLS
+    up, down = (row + ROWS - 1) & (ROWS - 1), (row + 1) & (ROWS - 1)
+    left, right = (col + COLS - 1) & (COLS - 1), (col + 1) & (COLS - 1)
     toward = [(down, col), (up, col), (row, right), (row, left), (down, right), (down, left), (up, right), (up, left)]
     reverse = [(up, col), (down, col), (row, left), (row, right), (up, left), (up, right), (down, left), (down, right)]
     bar = pltpu.get_barrier_semaphore()
-    for dev in toward:
+    for dev in toward[4:] + toward[:4]:
         pl.semaphore_signal(bar, inc=1, device_id=dev, device_id_type=MESH)
+    for i in FIRST:
+        loads[i].start()
     for axis in ("core", "x", "y", "z"):
         for _, dev in near[axis][1]:
             pl.semaphore_signal(bar, inc=1, device_id=dev, device_id_type=MESH)
@@ -211,7 +224,7 @@
             pltpu.make_async_remote_copy(
                 src_ref=s, dst_ref=t, send_sem=tsem_h.at[0, 8 * stage + i], recv_sem=tsem_h.at[1, 8 * stage + i],
                 device_id=dev, device_id_type=MESH)
-            for i, (dev, s, t) in enumerate(zip(devices, sources, targets))
+            for i, (dev, s, t) in reversed(list(enumerate(zip(devices, sources, targets))))
         ])
 
     def loaded(*names):
@@ -222,12 +235,6 @@
     pick = one_hot(slot_token(along(0, 96)), token_row)
     loaded(0)
     strips[...] = moved(pick, tokens[...])
-    order = one_hot(token_of(along(0, 128)), token_row)
-    feature = along(1, 256)
-    row_a[...] = one_hot(row_a_of(along(0, 256)), feature)
-    row_b[...] = one_hot(row_b_of(along(0, 128)), token_row)
-    ones_t[...] = one_hot(along(0, 256) >> 6, feature >> 6)
-    allowed[...] = allowed_keys(row, col)
     pl.semaphore_wait(bar, 8 + 1 + 3 + 7 + 7)
     spans = [pl.ds(0, 96), pl.ds(96, 96)] + [pl.ds(192 + 16 * s, 16) for s in range(6)]
     ch = halo(
@@ -236,9 +243,17 @@
         [xk.at[s] for s in spans],
     )
 
+
     loaded(6)
     dmx[7] = d_merged[...]
     cd = exchange(near["y"][1], lambda t: d_merged, dmx, tsem_d.at[0], tsem_d.at[1])
+
+    order = one_hot(token_of(along(0, 128)), token_row)
+    feature = along(1, 256)
+    row_a[...] = one_hot(row_a_of(along(0, 256)), feature)
+    row_b[...] = one_hot(row_b_of(along(0, 128)), token_row)
+    ones_t[...] = one_hot(along(0, 256) >> 6, feature >> 6)
+    allowed[...] = allowed_keys(row, col)
 
     loaded(1, 2, 3)
     ones = ones_t[...]
@@ -276,7 +291,8 @@
     for h in range(4):
         da4[128 * h : 128 * h + 128] = jnp.where(lane == h, d_attn, zero)
 
-    wait_copies(ch)
+
+    arrived(ch, sent)
     xh = xk[...].astype(F32)
     inverse_h, normed_h = norm_rows(xh, gains)
     kv_h = nn(normed_h, w_qkv[:, 256:])
@@ -329,14 +345,14 @@
     skip = (xp.astype(F32) + nn(attn, w_out[...])).astype(BF16)
     skips[...] = skip
     cb = exchange(
-        near["y"][1], lambda t: skips.at[mine(32, t // 2), mine(128, t % 2)], gx, tsem_b.at[0, :7], tsem_b.at[1, :7])
+        near["y"][1], lambda t: skips.at[mine(32, t >> 1), mine(128, t & 1)], gx, tsem_b.at[0, :7], tsem_b.at[1, :7])
 
     d_normed_h = nt(d_kraw[OWN:], w_qkv[:, 256:512]) + nt(d_v[OWN:], w_qkv[:, 512:])
     hs[...] = d_normed_h.astype(BF16)
-    ch = halo(1, reverse, [hs.at[s] for s in spans], [hr.at[s] for s in spans])
-    wait_copies(ca)
+    arrived(ca, sent)
     sa2[...] = (ga[mine(128, core)].astype(F32) + ra1[0].astype(F32)).astype(BF16)
     ca = exchange(near["x"][1], lambda t: sa2.at[mine(32, t)], ra2, *sems(tsem_a, 1))
+    ch = halo(1, reverse, [hs.at[s] for s in spans], [hr.at[s] for s in spans])
 
     d_normed = (nt(d_q, w_qkv[:, :256]) + nt(d_kraw[:OWN], w_qkv[:, 256:512])) + nt(d_v[:OWN], w_qkv[:, 512:])
     gain_row = jnp.sum(xhat[:OWN] * d_normed, axis=0, keepdims=True) + jnp.sum(
@@ -353,18 +369,18 @@
     o_merged[...] = nn(group, w_merge[...]).astype(BF16)
     saves[0].start()
     saves[1].start()
-    wait_copies(cg)
+    arrived(cg, sent)
     g2[x_at] = g1[0] + g1[1]
     cg = spread(x_at, near["x"][1], g2, *sems(tsem_g, 1))
 
-    gx[7] = skips[mine(32, y_at // 2), mine(128, y_at % 2)]
-    wait_copies(cd)
-    wait_copies(cb)
+    gx[7] = skips[mine(32, y_at >> 1), mine(128, y_at & 1)]
+    arrived(cd, sent)
+    arrived(cb, sent)
     factor = nt(row_b[...], gx[...].reshape(256, 128)).astype(BF16)
     gb[...] = nn(factor, dmx[...].reshape(256, 512)).astype(BF16)
     cb = exchange(near["core"][1], lambda t: gb.at[mine(64, t)], rb1, tsem_b.at[0, 7:8], tsem_b.at[1, 7:8])
 
-    wait_copies(ca)
+    arrived(ca, sent)
     total = sa2[mine(32, x_at)].astype(F32)
     for p in range(3):
         total = total + ra2[p].astype(F32)
@@ -373,14 +389,14 @@
          for c in range(4)], axis=0)
     sa3[...] = moved(one_hot(slab_of(along(0, 128)), token_row), total.astype(BF16)).reshape(8, 16, 256)
     ca = exchange(near["y"][1], lambda t: sa3.at[t], ra3, *sems(tsem_a, 2))
-    wait_copies(cg)
+    arrived(cg, sent)
     g3[y_at] = (g2[0] + g2[1]) + (g2[2] + g2[3])
     cg = spread(y_at, near["y"][1], g3, *sems(tsem_g, 2))
-    wait_copies(cb)
+    arrived(cb, sent)
     sb2[...] = (gb[mine(64, core)].astype(F32) + rb1[0].astype(F32)).astype(BF16)
     cb = exchange(near["x"][1], lambda t: sb2.at[mine(16, t)], rb2, tsem_b.at[0, 8:11], tsem_b.at[1, 8:11])
 
-    wait_copies(ch)
+    arrived(ch, sent)
     d_normed = d_normed + nn(one_hot(token_of(along(0, 128)), sent_token(along(1, HALO))), hr[...])
     scaled = gains * d_normed
     x = xp.astype(F32)
@@ -388,35 +404,39 @@
     o_tokens[...] = moved(unorder, (keep[2] + g_x).astype(BF16))
     saves[2].start()
 
-    wait_copies(cb)
+    arrived(cb, sent)
     total = sb2[mine(16, x_at)].astype(F32)
     for p in range(3):
         total = total + rb2[p].astype(F32)
     sb4[...] = total
     cb = exchange(
-        near["z"][1], lambda t: sb4.at[mine(8, t % 2), mine(128, t // 2)], rb4, tsem_b.at[0, 11:], tsem_b.at[1, 11:])
-
-    wait_copies(ca)
+        near["z"][1], lambda t: sb4.at[mine(8, t & 1), mine(128, t >> 1)], rb4, tsem_b.at[0, 11:], tsem_b.at[1, 11:])
+
+    arrived(ca, sent)
     total = sa3[y_at].astype(F32)
     for p in range(7):
         total = total + ra3[p].astype(F32)
     sa4[...] = total.reshape(2, 8, 256)
-    ca = exchange(near["z"][1], lambda t: sa4.at[t // 4], ra4, *sems(tsem_a, 3))
-    wait_copies(cg)
+    ca = exchange(near["z"][1], lambda t: sa4.at[t >> 2], ra4, *sems(tsem_a, 3))
+    arrived(cg, sent)
     g4[z_at] = ((g3[0] + g3[1]) + (g3[2] + g3[3])) + ((g3[4] + g3[5]) + (g3[6] + g3[7]))
     cg = spread(z_at, near["z"][1], g4, *sems(tsem_g, 3))
 
-    wait_copies(cb)
-    total = sb4[mine(8, z_at % 2), mine(128, z_at // 2)]
+    drain(sent)
+    for c in ca + cb + cg:
+        c.wait_send()
+    last = []
+    arrived(cb, last)
+    total = sb4[mine(8, z_at & 1), mine(128, z_at >> 1)]
     for p in range(7):
         total = total + rb4[p]
     o_merge[...] = total
     saves[5].start()
-    wait_copies(ca)
-    total = sa4[z_at // 4]
+    arrived(ca, last)
+    total = sa4[z_at >> 2]
     for p in range(7):
         total = total + ra4[p]
-    part = z_at % 4
+    part = z_at & 3
     piece = jnp.zeros((2, 256), F32)
     for i in range(4):
         piece = piece + jnp.where(part == i, total[2 * i : 2 * i + 2], 0.0)
@@ -424,7 +444,7 @@
     o_out[...] = piece[:, 192:]
     saves[3].start()
     saves[4].start()
-    wait_copies(cg)
+    arrived(cg, last)
     total = ((g4[0] + g4[1]) + (g4[2] + g4[3])) + ((g4[4] + g4[5]) + (g4[6] + g4[7]))
     o_gain[...] = total[0:2]
     halves = lax.broadcasted_iota(jnp.int32, (1, 128), 1)

time: 45.8 us -> 44.1 us (0.963); the launches traced: 45 us -> 43.9 us
  Pallas kernels: 44.3 us -> 43.2 us
    pallas_call x1, Pallas kernels: 42.6 us -> 41.6 us  [on_device(): pl.pallas_call(body, out_shape=results, in_specs=[far] * 8, out_specs=(fa...]
where the time goes in v5:
time: 44.1 us; the launch traced here: 43.9 us
  Pallas kernels  43.2 us (98%)
  between operations  0.64 us (1%)
    pallas_call x1, Pallas kernels, on_device(): pl.pallas_call(body, out_shape=results, in_specs=[far] * 8, out_specs=(fa...  41.6 us
    pallas_call x1, Pallas kernels, on_device(): pl.pallas_call(hand_over, out_shape=results, in_specs=[far] * 8, out_spec...  1.67 us

profile of v5, /device:TPU:6, one launch (start us, length us, event | category | flops | bytes accessed | tf_op | source)
XLA Modules:
  0.0 43.9 jit_solution(11451295989599305025)
XLA Ops:
  0.6 41.6 %shard_map.143 = (bf16[128,256]{1,0:T(8,128)(2,1)}, bf16[32,512]{1,0:T(8,128)(2,1)}, bf16[128,256]{1,0:T(8,128)(2,1)}, f32[2,192]{1,0:T(2,128)}, f32[2,64]{1,0:T...) custom-call(bf16[128,256]{1,0:T(8,128)(2,1)} %bitcast.10, f32[1,256]{1,0:T(1,128)} %bitcast.13, ...), custom_call_target="tpu_custom_call" | custom-call | tf_op jit(solution)/shard_map/pallas_call | solution.py:484
  42.2 1.7 %shard_map.144 = (bf16[128,256]{1,0:T(8,128)(2,1)}, bf16[32,512]{1,0:T(8,128)(2,1)}, bf16[128,256]{1,0:T(8,128)(2,1)}, f32[2,192]{1,0:T(2,128)}, f32[2,64]{1,0:T...) custom-call(bf16[128,256]{1,0:T(8,128)(2,1)} %get-tuple-element.24.refs_0_, ...), custom_call_target="tpu_custom_call" | custom-call | tf_op jit(solution)/shard_map/pallas_call | solution.py:509

commit v6 on v5

--- a/solution.py
+++ b/solution.py
@@ -195,7 +195,7 @@
 
 def compute(loads, saves, tokens, gain, w_qkv, head_scale, w_out, w_merge, d_merged, d_skip,
          o_skip, o_merged, o_tokens, o_qkv, o_out, o_merge, o_gain, o_scale,
-         xk, strips, row_a, row_b, ones_t, kv, kvt, st, pt, ptb, dst, q4, da4, keep, keys, xhat, nt_all, hs, hr, allowed,
+         xk, strips, row_a, row_b, ones_t, kv, kvt, st, dwt, ptb, dst, q4, da4, keep, keys, xhat, nt_all, hs, hr, allowed,
          ga, ra1, sa2, ra2, sa3, ra3, sa4, ra4,
          skips, gx, dmx, gb, rb1, sb2, rb2, sb4, rb4,
          g1, g2, g3, g4, tsem_a, tsem_b, tsem_d, tsem_g, tsem_h):
@@ -292,6 +292,15 @@
         da4[128 * h : 128 * h + 128] = jnp.where(lane == h, d_attn, zero)
 
 
+    st[:OWN] = nt(kv[:OWN, :256], q4[...])
+    dwt[:OWN] = nt(kv[:OWN, 256:], da4[...])
+    for h in range(4):
+        span = slice(128 * h, 128 * h + 128)
+        st[:OWN, span] = jnp.exp(st[:OWN, span]) * allowed[:OWN]
+    eye = one_hot(along(0, 256), feature)
+    kvt[:256, :OWN] = nt(eye, kv[:OWN, :256]).astype(BF16)
+    kvt[256:, :OWN] = nt(eye, kv[:OWN, 256:]).astype(BF16)
+
     arrived(ch, sent)
     xh = xk[...].astype(F32)
     inverse_h, normed_h = norm_rows(xh, gains)
@@ -303,28 +312,29 @@
     kv[OWN:, :256] = k_unit_h.astype(BF16)
     kv[OWN:, 256:] = kv_h[:, 256:].astype(BF16)
 
-    st[...] = nt(kv[:, :256], q4[...])
+    st[OWN:] = nt(kv[OWN:, :256], q4[...])
+    dwt[OWN:] = nt(kv[OWN:, 256:], da4[...])
     for h in range(4):
         span = slice(128 * h, 128 * h + 128)
-        e = jnp.exp(st[:, span]) * allowed[...]
-        p = e * (1.0 / jnp.sum(e, axis=0, keepdims=True))
-        pt[:, span] = p
-        ptb[:, span] = p.astype(BF16)
-
-    st[...] = nt(kv[:, 256:], da4[...])
-    for h in range(4):
-        span = slice(128 * h, 128 * h + 128)
-        dw, p = st[:, span], pt[:, span]
-        dst[:, span] = (p * (dw - jnp.sum(dw * p, axis=0, keepdims=True))).astype(BF16)
+        e = jnp.exp(st[OWN:, span]) * allowed[OWN:]
+        own = st[:OWN, span]
+        r = 1.0 / (jnp.sum(own, axis=0, keepdims=True) + jnp.sum(e, axis=0, keepdims=True))
+        p, p_own = e * r, own * r
+        ptb[:OWN, span] = p_own.astype(BF16)
+        ptb[OWN:, span] = p.astype(BF16)
+
+        dw, dw_own = dwt[OWN:, span], dwt[:OWN, span]
+        mean = jnp.sum(dw * p, axis=0, keepdims=True) + jnp.sum(dw_own * p_own, axis=0, keepdims=True)
+        dst[:OWN, span] = (p_own * (dw_own - mean)).astype(BF16)
+        dst[OWN:, span] = (p * (dw - mean)).astype(BF16)
     d_k = nn(dst[...], q4[...])
     ku = keys[1]
     d_kraw = (keys[0] * (d_k - ku * head_sums(ku * d_k, ones))).astype(BF16)
     d_v = nn(ptb[...], da4[...]).astype(BF16)
     nt_all[:, OWN:] = nt(row_a[...], normed_h).astype(BF16)
     normed_t = nt_all[...]
-    eye = one_hot(along(0, 256), feature)
-    kvt[:256] = nt(eye, kv[:, :256]).astype(BF16)
-    kvt[256:] = nt(eye, kv[:, 256:]).astype(BF16)
+    kvt[:256, OWN:] = nt(eye, kv[OWN:, :256]).astype(BF16)
+    kvt[256:, OWN:] = nt(eye, kv[OWN:, 256:]).astype(BF16)
 
     def diagonal(full):
         return jnp.concatenate([full[64 * h : 64 * h + 64, 128 * h : 128 * h + 128] for h in range(4)], axis=0)

time: 44.1 us -> 44.3 us (level)
  no operation moved by 1% of the time
where the time goes in v6:
time: 44.3 us; the launch traced here: 44.1 us
  Pallas kernels  43.5 us (98%)
  between operations  0.64 us (1%)
    pallas_call x1, Pallas kernels, on_device(): pl.pallas_call(body, out_shape=results, in_specs=[far] * 8, out_specs=(fa...  41.8 us
    pallas_call x1, Pallas kernels, on_device(): pl.pallas_call(hand_over, out_shape=results, in_specs=[far] * 8, out_spec...  1.67 us

profile of v6, /device:TPU:6, one launch (start us, length us, event | category | flops | bytes accessed | tf_op | source)
XLA Modules:
  0.0 44.1 jit_solution(14382404956225988456)
XLA Ops:
  0.6 41.8 %shard_map.143 = (bf16[128,256]{1,0:T(8,128)(2,1)}, bf16[32,512]{1,0:T(8,128)(2,1)}, bf16[128,256]{1,0:T(8,128)(2,1)}, f32[2,192]{1,0:T(2,128)}, f32[2,64]{1,0:T...) custom-call(bf16[128,256]{1,0:T(8,128)(2,1)} %bitcast.10, f32[1,256]{1,0:T(1,128)} %bitcast.13, ...), custom_call_target="tpu_custom_call" | custom-call | tf_op jit(solution)/shard_map/pallas_call | solution.py:494
  42.4 1.7 %shard_map.144 = (bf16[128,256]{1,0:T(8,128)(2,1)}, bf16[32,512]{1,0:T(8,128)(2,1)}, bf16[128,256]{1,0:T(8,128)(2,1)}, f32[2,192]{1,0:T(2,128)}, f32[2,64]{1,0:T...) custom-call(bf16[128,256]{1,0:T(8,128)(2,1)} %get-tuple-element.24.refs_0_, ...), custom_call_target="tpu_custom_call" | custom-call | tf_op jit(solution)/shard_map/pallas_call | solution.py:519
